TPU v7x, 32 devices: a whole 2x2x4 slice. The times are simulated.
32 devices in a mesh: dp: 2 (over core), tm: 4 (over z), space: 4 (over y, x).
Axes of the slice: x: 2, y: 2, z: 4, core: 2. Of those that a mesh axis runs over, the one named last changes fastest.
Arguments:
- latents: bfloat16 [2, 8, 8, 80, 512], P('dp', 'tm', 'space'), may hold values from -6 to 6
- norm_gain: float32 [512], replicated, may hold values from 0.25 to 1.75
- kernel: bfloat16 [13824, 512], P(None, 'dp'), may hold values from -0.0546875 to 0.0546875
- conv_bias: float32 [512], replicated, may hold values from -3 to 3
- out_grad: bfloat16 [2, 8, 8, 80, 512], P('dp', 'tm', 'space'), may hold values from -6 to 6
Outputs:
- block_out: bfloat16 [2, 8, 8, 80, 512], P('dp', 'tm', 'space')
- latent_grad: bfloat16 [2, 8, 8, 80, 512], P('dp', 'tm', 'space')
- kernel_grad: float32 [13824, 512], P('tm', 'dp')
- gain_grad: float32 [512], replicated
- bias_grad: float32 [512], replicated
All inputs are finite; a program needn't handle non-finite values.
Results may differ from a plain program's by a relative error of at most 0.0029.
Values may be sent and summed in bfloat16 or wider, within the bound.
A program may use at most 128 MiB of HBM per device.

v0:
```python
import jax
import jax.numpy as jnp
from jax import lax
from jax.sharding import PartitionSpec as P


def shifted(block, axis, distance):
    devices = range(lax.axis_size(axis))
    route = [(i - distance, i) for i in devices if i - distance in devices]
    return lax.ppermute(block, axis, route)


def padded(block, sides, width):
    for axis, dim in sides:
        count = lax.axis_size(axis)
        forward = [(i, i + 1) for i in range(count - 1)]
        backward = [(target, source) for source, target in forward]
        low = lax.ppermute(
            lax.slice_in_dim(block, block.shape[dim] - width, None, axis=dim), axis, forward
        )
        high = lax.ppermute(lax.slice_in_dim(block, 0, width, axis=dim), axis, backward)
        block = jnp.concatenate([low, block, high], axis=dim)
    return block


def tap_columns(extended, frame_count, row_count, col_count, flipped):
    pieces = []
    for tap_t in range(3):
        for tap_h in range(3):
            for tap_w in range(3):
                if flipped:
                    start_t, start_h, start_w = (2 - tap_t, 2 - tap_h, 2 - tap_w)
                else:
                    start_t, start_h, start_w = (tap_t, tap_h, tap_w)
                pieces.append(
                    extended[
                        :,
                        start_t : start_t + frame_count,
                        start_h : start_h + row_count,
                        start_w : start_w + col_count,
                        :,
                    ]
                )
    stacked = jnp.concatenate(pieces, axis=-1)
    return stacked.reshape(-1, stacked.shape[-1])


def pad_columns(extended):
    return jnp.pad(extended, ((0, 0), (0, 0), (0, 0), (1, 1), (0, 0)))


def on_device(latents, norm_gain, kernel, conv_bias, out_grad):
    chans = latents.shape[-1]
    half_cols = kernel.shape[1]
    clip_local, frame_count, row_count, col_count = (
        latents.shape[0],
        latents.shape[1],
        latents.shape[2],
        latents.shape[3],
    )
    cell_total = (
        clip_local
        * frame_count
        * row_count
        * col_count
        * lax.axis_size("dp")
        * lax.axis_size("tm")
        * lax.axis_size("space")
    )
    grad_scale = 1.0 / jnp.sqrt(jnp.float32(cell_total))
    floats = latents.astype(jnp.float32)
    scale = lax.rsqrt(jnp.mean(floats * floats, axis=-1, keepdims=True) + 1e-06)
    normed = floats * scale
    pre_act = normed * norm_gain
    act = jax.nn.silu(pre_act).astype(jnp.bfloat16)
    grad_pair = lax.all_to_all(out_grad, "dp", split_axis=4, concat_axis=0, tiled=True)
    earlier = shifted(act, "tm", 1)
    joined = jnp.concatenate([earlier, act], axis=1)
    act_ext = padded(joined, (("space", 2),), 1)
    later = shifted(grad_pair, "tm", -1)
    joined_grad = jnp.concatenate([grad_pair, later], axis=1)
    grad_ext = padded(joined_grad, (("space", 2),), 1)
    act_pair = lax.all_gather(act_ext, "dp", axis=0, tiled=True)
    pair_clips = act_pair.shape[0]
    act_taps = tap_columns(pad_columns(act_pair), frame_count, row_count, col_count, False)
    conv_part = jnp.dot(act_taps, kernel, preferred_element_type=jnp.float32)
    conv_part = conv_part.reshape(pair_clips, frame_count, row_count, col_count, half_cols)
    conv = lax.all_to_all(conv_part, "dp", split_axis=0, concat_axis=4, tiled=True)
    block_out = (floats + conv + conv_bias).astype(jnp.bfloat16)
    kernel_local = (
        lax.dot_general(
            act_taps,
            grad_pair.reshape(-1, half_cols),
            (((0,), (0,)), ((), ())),
            preferred_element_type=jnp.float32,
        )
        * grad_scale
    )
    flipped_kernel = jnp.transpose(kernel.reshape(-1, chans, half_cols), (0, 2, 1)).reshape(
        -1, chans
    )
    grad_taps = tap_columns(pad_columns(grad_ext), frame_count, row_count, col_count, True)
    partial_grad = jnp.dot(grad_taps, flipped_kernel, preferred_element_type=jnp.float32)
    partial_grad = partial_grad.reshape(pair_clips, frame_count, row_count, col_count, chans)
    act_grad = lax.psum_scatter(partial_grad, "dp", scatter_dimension=0, tiled=True)
    grads = out_grad.astype(jnp.float32)
    bias_local = jnp.sum(grads.reshape(-1, chans), axis=0) * grad_scale
    sig = jax.nn.sigmoid(pre_act)
    pre_grad = act_grad * sig * (1.0 + pre_act * (1.0 - sig))
    gain_local = jnp.sum((pre_grad * normed).reshape(-1, chans), axis=0) * grad_scale
    normed_grad = pre_grad * norm_gain
    latent_grad = grads + scale * (
        normed_grad - normed * jnp.mean(normed_grad * normed, axis=-1, keepdims=True)
    )
    gain_grad, bias_grad = lax.psum((gain_local, bias_local), ("dp", "tm", "space"))
    col_part = lax.psum_scatter(kernel_local, "space", scatter_dimension=1, tiled=True)
    cell_part = lax.psum_scatter(col_part, "tm", scatter_dimension=0, tiled=True)
    kernel_grad = lax.all_gather(cell_part, "space", axis=1, tiled=True)
    return (block_out, latent_grad.astype(jnp.bfloat16), kernel_grad, gain_grad, bias_grad)


def solution(mesh):
    in_specs = (
        P("dp", "tm", "space", None, None),
        P(),
        P(None, "dp"),
        P(),
        P("dp", "tm", "space", None, None),
    )
    out_specs = (
        P("dp", "tm", "space", None, None),
        P("dp", "tm", "space", None, None),
        P("tm", "dp"),
        P(),
        P(),
    )
    return jax.shard_map(
        on_device, mesh=mesh, in_specs=in_specs, out_specs=out_specs, check_vma=False
    )
```

profile of v0, /device:TPU:0, one launch (start us, length us, event | category | flops | bytes accessed | tf_op | source)
XLA Modules:
  0.0 405.0 jit_solution(16360685928607318187)
XLA Ops:
  8.5 4.2 %all_to_all.36 = bf16[1,2,2,80,512]{3,2,1,0,4:T(2,128)(2,1)S(1)} all-to-all(bf16[1,2,2,80,512]{3,2,1,0,4:T(2,128)(2,1)S(1)} %copy.23), channel_id=1, replica_groups=mesh['dp'=2,'tm'=4,'space'=4] {'dp'}, dimensions={4} | all-to-all | bytes 655360 | tf_op jit(solution)/shard_map/all_to_all | solution.py:76
  14.3 11.6 %collective-permute-done.3 = bf16[2,2,2,80,256]{4,3,2,1,0:T(8,128)(2,1)S(1)} collective-permute-done((bf16[2,2,2,80,256]{4,3,2,1,0:T(8,128)(2,1)S(1)}, bf16[2,2,2,80,256]{4,3,2,1,0:T(8,128)(2,1)S(1)}, u32[]{:S(2)}, u32[]{:S(2)}) %collective-permute-start.3) | collective-permute-done | bytes 327712 | tf_op jit(solution)/shard_map/ppermute | solution.py:10
  26.0 3.6 collective-permute-start.4
  30.9 10.3 %copy.26 = bf16[27,256,512]{2,1,0:T(8,128)(2,1)} copy(bf16[27,256,512]{1,2,0:T(8,128)(2,1)} %bitcast.38) | data formatting | bytes 14155776 | tf_op jit(solution)/shard_map/transpose | solution.py:99
  41.2 3.8 collective-permute-done.5
  49.2 5.8 %fusion.31 = f32[2,2,2,80,512]{4,3,2,1,0:T(8,128)} fusion(bf16[2,2,2,80,6912]{4,3,2,1,0:T(8,128)(2,1)S(1)} %slice_dynamic-update-slice_fusion.27, bf16[6912,512,1,1,1]{1,0,4,3,2:T(8,128)(2,1)S(1)} %bitcast.41), kind=kOutput, calls=%fused_computation.109 | convolution fusion | flops 4529848320 | bytes 17235968 | tf_op jit(solution)/shard_map/dot_general | solution.py:103
  55.2 8.0 %reduce-scatter.4.cloned.1.call-done = f32[1,2,2,80,512]{4,3,2,1,0:T(8,128)} async-done(((f32[2,2,2,80,512]{4,3,2,1,0:T(8,128)}), f32[1,2,2,80,512]{4,3,2,1,0:T(8,128)}) %reduce-scatter.4.cloned.1.call-update) | async-done | bytes 655376 | tf_op jit(solution)/shard_map/reduce_scatter | solution.py:105
  63.2 1.6 fusion.23
  64.9 2.4 fusion.13
  67.2 3.7 collective-permute-start
  70.9 7.4 %collective-permute-done = bf16[1,2,2,80,512]{4,3,2,1,0:T(8,128)(2,1)S(1)} collective-permute-done((bf16[1,2,2,80,512]{4,3,2,1,0:T(8,128)(2,1)S(1)}, bf16[1,2,2,80,512]{4,3,2,1,0:T(8,128)(2,1)S(1)}, u32[]{:S(2)}, u32[]{:S(2)}) %collective-permute-start) | collective-permute-done | bytes 327712 | tf_op jit(solution)/shard_map/ppermute | solution.py:10
  78.3 3.4 collective-permute-start.1
  83.0 5.2 %collective-permute-done.1 = bf16[1,4,1,80,512]{4,3,2,1,0:T(8,128)(2,1)S(1)} collective-permute-done((bf16[1,4,1,80,512]{4,3,2,1,0:T(8,128)(2,1)S(1)}, bf16[1,4,1,80,512]{4,3,2,1,0:T(8,128)(2,1)S(1)}, u32[]{:S(2)}, u32[]{:S(2)}) %collective-permute-start.1) | collective-permute-done | bytes 327712 | tf_op jit(solution)/shard_map/ppermute | solution.py:18
  88.3 9.0 %collective-permute-done.2 = bf16[1,4,1,80,512]{4,3,2,1,0:T(8,128)(2,1)S(1)} collective-permute-done((bf16[1,4,1,80,512]{4,3,2,1,0:T(8,128)(2,1)S(1)}, bf16[1,4,1,80,512]{4,3,2,1,0:T(8,128)(2,1)S(1)}, u32[]{:S(2)}, u32[]{:S(2)}) %collective-permute-start.2) | collective-permute-done | bytes 327712 | tf_op jit(solution)/shard_map/ppermute | solution.py:21
  98.7 12.3 %all-gather.3.cloned.1.call-done = bf16[2,4,4,80,512]{4,3,2,1,0:T(8,128)(2,1)} async-done(((bf16[1,4,4,80,512]{4,3,2,1,0:T(8,128)(2,1)}), bf16[2,4,4,80,512]{4,3,2,1,0:T(8,128)(2,1)}) %all-gather.3.cloned.1.call-update) | async-done | bytes 2621456 | tf_op jit(solution)/shard_map/all_gather | solution.py:83
  111.0 1.4 slice_dynamic-update-slice_fusion.26
  117.9 6.0 %copy-done.1 = bf16[2,2,2,80,13824]{4,3,2,1,0:T(8,128)(2,1)} copy-done((bf16[2,2,2,80,13824]{4,3,2,1,0:T(8,128)(2,1)}, bf16[2,2,2,80,13824]{4,3,2,1,0:T(8,128)(2,1)S(1)}, u32[]{:S(2)}) %copy-start.1) | copy-done | bytes 17694744
  123.9 9.1 %convolution_multiply_fusion = f32[13824,256]{0,1:T(8,128)} fusion(bf16[640,13824]{1,0:T(8,128)(2,1)S(1)} %bitcast.31, bf16[640,256]{1,0:T(8,128)(2,1)S(1)} %bitcast.37), kind=kOutput, calls=%fused_computation | convolution fusion | flops 4533387264 | bytes 32178176 | tf_op jit(solution)/shard_map/dot_general | solution.py:91
  133.1 134.9 %reduce-scatter.6.cloned.1.call-done = f32[13824,64]{0,1:T(8,128)} async-done(((f32[13824,256]{0,1:T(8,128)}), f32[13824,64]{0,1:T(8,128)}) %reduce-scatter.6.cloned.1.call-update) | async-done | bytes 3538960 | tf_op jit(solution)/shard_map/reduce_scatter | solution.py:116
  268.0 68.6 %reduce-scatter.8.cloned.1.call-done = f32[3456,64]{0,1:T(8,128)} async-done(((f32[13824,64]{0,1:T(8,128)}), f32[3456,64]{0,1:T(8,128)}) %reduce-scatter.8.cloned.1.call-update) | async-done | bytes 884752 | tf_op jit(solution)/shard_map/reduce_scatter | solution.py:117
  336.7 41.0 %all-reduce.2 = (f32[512]{0:T(512)}, f32[512]{0:T(512)}) all-reduce(f32[512]{0:T(512)S(1)} %broadcast_multiply_fusion.1, f32[512]{0:T(512)S(1)} %broadcast_multiply_fusion), channel_id=1, replica_groups=mesh['dp'=2,'tm'=4,'space'=4] {'dp','tm','space'}, use_global_device_ids=true, to_apply=%region_6.7 | all-reduce | flops 1024 | bytes 8192 | tf_op jit(solution)/shard_map/psum | solution.py:115
  377.6 10.5 %fusion = f32[2,2,2,80,256]{4,3,2,1,0:T(8,128)S(1)} fusion(bf16[2,2,2,80,13824]{4,3,2,1,0:T(8,128)(2,1)} %copy-done.1, bf16[13824,256]{1,0:T(8,128)(2,1)} %param.7), kind=kOutput, calls=%fused_computation.1 | convolution fusion | flops 4529848320 | bytes 25427968 | tf_op jit(solution)/shard_map/dot_general | solution.py:86
  388.1 4.3 %all_to_all.37 = f32[2,2,2,80,256]{4,3,2,1,0:T(8,128)S(1)} all-to-all(f32[2,2,2,80,256]{4,3,2,1,0:T(8,128)S(1)} %fusion), channel_id=1, replica_groups=mesh['dp'=2,'tm'=4,'space'=4] {'dp'}, dimensions={0} | all-to-all | bytes 1310720 | tf_op jit(solution)/shard_map/all_to_all | solution.py:88
  393.3 5.2 %copy.27 = f32[3456,256]{1,0:T(8,128)} copy(f32[3456,256]{0,1:T(8,128)} %all-gather.5.cloned.1.call-done) | data formatting | bytes 7077888
  (98 shorter events, 17.6 us)
Async XLA Ops:
  7.2 56.1 %reduce-scatter.4.cloned.1.call-start = ((), (), s32[]{:S(2)}) async-start(), calls=%async_computation.6 | async-start | bytes 1966080 | tf_op jit(solution)/shard_map/reduce_scatter | solution.py:105
  13.0 12.9 %collective-permute-start.3 = (bf16[2,2,2,80,256]{4,3,2,1,0:T(8,128)(2,1)S(1)}, bf16[2,2,2,80,256]{4,3,2,1,0:T(8,128)(2,1)S(1)}, u32[]{:S(2)}, u32[]{:S(2)}) collective-permute-start(bf16[2,2,2,80,256]{4,3,2,1,0:T(8,128)(2,1)S(1)} %bitcast.32), channel_id=1, source_target_pairs={{4,0},{8,4},{12,8},{5,1},{9,5},{13,9},{6,2},{10,6},{14,10},{7,3},{... | collective-permute-start | bytes 983048 | tf_op jit(solution)/shard_map/ppermute | solution.py:10
  26.0 15.2 %collective-permute-start.4 = (bf16[2,4,1,80,256]{4,3,2,1,0:T(8,128)(2,1)S(1)}, bf16[2,4,1,80,256]{4,3,2,1,0:T(8,128)(2,1)S(1)}, u32[]{:S(2)}, u32[]{:S(2)}) collective-permute-start(bf16[2,4,1,80,256]{4,3,2,1,0:T(8,128)(2,1)S(1)} %get-tuple-element.31), channel_id=1, source_target_pairs={{0,1},{1,2},{2,3},{4,5},{5,6},{6,7},{8,9},{9,10},{10,11},{12,13},{... | collective-permute-start | bytes 983048 | tf_op jit(solution)/shard_map/ppermute | solution.py:18
  29.6 15.4 %collective-permute-start.5 = (bf16[2,4,1,80,256]{4,3,2,1,0:T(8,128)(2,1)S(1)}, bf16[2,4,1,80,256]{4,3,2,1,0:T(8,128)(2,1)S(1)}, u32[]{:S(2)}, u32[]{:S(2)}) collective-permute-start(bf16[2,4,1,80,256]{4,3,2,1,0:T(8,128)(2,1)S(1)} %get-tuple-element.32), channel_id=1, source_target_pairs={{1,0},{2,1},{3,2},{5,4},{6,5},{7,6},{9,8},{10,9},{11,10},{13,12},{... | collective-permute-start | bytes 983048 | tf_op jit(solution)/shard_map/ppermute | solution.py:21
  45.9 2.2 slice-start
  46.6 2.6 slice-start.1
  49.2 5.9 %copy-start.2 = (bf16[1,2,2,80,512]{4,3,2,1,0:T(8,128)(2,1)S(1)}, bf16[1,2,2,80,512]{4,3,2,1,0:T(8,128)(2,1)}, u32[]{:S(2)}) copy-start(bf16[1,2,2,80,512]{4,3,2,1,0:T(8,128)(2,1)} %param.5) | copy-start | bytes 983044
  49.2 14.0 %copy-start.4 = (f32[512]{0:T(512)S(1)}, f32[512]{0:T(512)}, u32[]{:S(2)}) copy-start(f32[512]{0:T(512)} %param.6) | copy-start | bytes 6148
  49.2 15.7 %copy-start.3 = (bf16[1,2,2,80,512]{4,3,2,1,0:T(8,128)(2,1)S(1)}, bf16[1,2,2,80,512]{4,3,2,1,0:T(8,128)(2,1)}, u32[]{:S(2)}) copy-start(bf16[1,2,2,80,512]{4,3,2,1,0:T(8,128)(2,1)} %param.9) | copy-start | bytes 983044
  55.0 56.0 %all-gather.3.cloned.1.call-start = ((), (), s32[]{:S(2)}) async-start(), calls=%async_computation.5 | async-start | bytes 3932160 | tf_op jit(solution)/shard_map/all_gather | solution.py:83
  67.2 11.1 %collective-permute-start = (bf16[1,2,2,80,512]{4,3,2,1,0:T(8,128)(2,1)S(1)}, bf16[1,2,2,80,512]{4,3,2,1,0:T(8,128)(2,1)S(1)}, u32[]{:S(2)}, u32[]{:S(2)}) collective-permute-start(bf16[1,2,2,80,512]{4,3,2,1,0:T(8,128)(2,1)S(1)} %get-tuple-element.36), channel_id=1, source_target_pairs={{0,4},{4,8},{8,12},{1,5},{5,9},{9,13},{2,6},{6,10},{10,14},{3,7},{... | collective-permute-start | bytes 983048 | tf_op jit(solution)/shard_map/ppermute | solution.py:10
  78.3 9.9 %collective-permute-start.1 = (bf16[1,4,1,80,512]{4,3,2,1,0:T(8,128)(2,1)S(1)}, bf16[1,4,1,80,512]{4,3,2,1,0:T(8,128)(2,1)S(1)}, u32[]{:S(2)}, u32[]{:S(2)}) collective-permute-start(bf16[1,4,1,80,512]{4,3,2,1,0:T(8,128)(2,1)S(1)} %get-tuple-element.33), channel_id=1, source_target_pairs={{0,1},{1,2},{2,3},{4,5},{5,6},{6,7},{8,9},{9,10},{10,11},{12,13},{... | collective-permute-start | bytes 983048 | tf_op jit(solution)/shard_map/ppermute | solution.py:18
  81.7 15.5 %collective-permute-start.2 = (bf16[1,4,1,80,512]{4,3,2,1,0:T(8,128)(2,1)S(1)}, bf16[1,4,1,80,512]{4,3,2,1,0:T(8,128)(2,1)S(1)}, u32[]{:S(2)}, u32[]{:S(2)}) collective-permute-start(bf16[1,4,1,80,512]{4,3,2,1,0:T(8,128)(2,1)S(1)} %get-tuple-element.34), channel_id=1, source_target_pairs={{1,0},{2,1},{3,2},{5,4},{6,5},{7,6},{9,8},{10,9},{11,10},{13,12},{... | collective-permute-start | bytes 983048 | tf_op jit(solution)/shard_map/ppermute | solution.py:21
  98.5 169.4 %reduce-scatter.6.cloned.1.call-start = ((), (), s32[]{:S(2)}) async-start(), calls=%async_computation.7 | async-start | bytes 17694720 | tf_op jit(solution)/shard_map/reduce_scatter | solution.py:116
  111.0 3.8 copy-start
  117.9 6.1 %copy-start.1 = (bf16[2,2,2,80,13824]{4,3,2,1,0:T(8,128)(2,1)}, bf16[2,2,2,80,13824]{4,3,2,1,0:T(8,128)(2,1)S(1)}, u32[]{:S(2)}) copy-start(bf16[2,2,2,80,13824]{4,3,2,1,0:T(8,128)(2,1)S(1)} %slice_dynamic-update-slice_fusion.9) | copy-start | bytes 53084164
  133.0 203.6 %reduce-scatter.8.cloned.1.call-start = ((), (), s32[]{:S(2)}) async-start(), calls=%async_computation.8 | async-start | bytes 4423680 | tf_op jit(solution)/shard_map/reduce_scatter | solution.py:117
  268.0 125.3 %all-gather.5.cloned.1.call-start = ((), (), s32[]{:S(2)}) async-start(), calls=%async_computation.9 | async-start | bytes 4423680 | tf_op jit(solution)/shard_map/all_gather | solution.py:118
  377.6 14.9 %copy-start.5 = (f32[512]{0:T(512)S(1)}, f32[512]{0:T(512)}, u32[]{:S(2)}) copy-start(f32[512]{0:T(512)} %param.8) | copy-start | bytes 6148
Sparse Core Ops, SparseCore 0:
  55.1 8.0 reduce-scatter.3
  98.6 12.3 all-gather.2
  133.1 134.7 reduce-scatter.5
  270.2 66.3 reduce-scatter.7
  338.5 48.2 all-gather.4
where the time goes:
time: 406 us; the launch traced here: 405 us
  waiting for transfers between devices  261 us (64%)
  blocking collectives  49.4 us (12%)
  local copies, waits for them, and re-layouts  33 us (8%)
  matrix products  25.4 us (6%)
  starting transfers between devices  14.9 us (4%)
  between operations  14.4 us (4%)
  other arithmetic  7.21 us (2%)
    reduce_scatter x1, waiting for transfers between devices, on_device(): lax.psum_scatter(kernel_local, 'space', scatter_dimension=1, tiled=True)  135 us
    reduce_scatter x1, waiting for transfers between devices, on_device(): lax.psum_scatter(col_part, 'tm', scatter_dimension=0, tiled=True)  68.6 us
    psum x1, blocking collectives, on_device(): lax.psum((gain_local, bias_local), ('dp', 'tm', 'space'))  41 us
    unnamed x69, local copies, waits for them, and re-layouts  22 us
    ppermute x2, waiting for transfers between devices, shifted(): return lax.ppermute(block, axis, route)  19 us
    ppermute x2, waiting for transfers between devices, padded(): lax.ppermute(lax.slice_in_dim(block, 0, width, axis=dim), axis, backward)  12.7 us
    all_gather x1, waiting for transfers between devices, on_device(): act_pair = lax.all_gather(act_ext, 'dp', axis=0, tiled=True)  12.3 us
    dot_general x1, matrix products, on_device(): conv_part = jnp.dot(act_taps, kernel, preferred_element_type=jnp.float32)  10.5 us
  transfers between devices with their start and end apart: 11, of which 9 were waited for; matrix products, arithmetic and copies ran while one was open for 5% of the time, Pallas kernels for 0%

commit v1 on v0

--- a/solution.py
+++ b/solution.py
@@ -1,6 +1,10 @@
+import functools
+
 import jax
 import jax.numpy as jnp
 from jax import lax
+from jax.experimental import pallas as pl
+from jax.experimental.pallas import tpu as pltpu
 from jax.sharding import PartitionSpec as P
 
 
@@ -49,6 +53,183 @@
     return jnp.pad(extended, ((0, 0), (0, 0), (0, 0), (1, 1), (0, 0)))
 
 
+MESH = pl.DeviceIdType.MESH
+
+
+def first_tap(owner, quarter, per, parts):
+    return (per * owner - quarter + parts - 1) // parts
+
+
+def reduce_spread_kernel(
+    n, parts, per, slots, part_ref, out_ref, from_left, from_right, to_right, to_left, done,
+    right_send, right_recv, left_send, left_recv, spread_send, spread_recv, own_sem,
+):
+    me_d, me_t, me_s = lax.axis_index("dp"), lax.axis_index("tm"), lax.axis_index("space")
+    barrier = pltpu.get_barrier_semaphore()
+
+    def signal(t, s):
+        pl.semaphore_signal(barrier, inc=1, device_id=(me_d, t, s), device_id_type=MESH)
+
+    for other in range(1, parts):
+        signal(me_t, lax.rem(me_s + other, parts))
+
+    @pl.when(me_t > 0)
+    def _():
+        signal(me_t - 1, me_s)
+
+    @pl.when(me_t < n - 1)
+    def _():
+        signal(me_t + 1, me_s)
+
+    ends = jnp.where(me_t > 0, 1, 0) + jnp.where(me_t < n - 1, 1, 0)
+    pl.semaphore_wait(barrier, parts - 1 + ends)
+
+    def mine(dest, slot):
+        return part_ref[first_tap(dest, me_s, per, parts) + slot]
+
+    def right_copy(dest, slot, target):
+        return pltpu.make_async_remote_copy(
+            src_ref=to_right.at[dest, slot], dst_ref=from_left.at[dest, slot],
+            send_sem=right_send.at[dest, slot], recv_sem=right_recv.at[dest, slot],
+            device_id=(me_d, target, me_s), device_id_type=MESH)
+
+    def left_copy(dest, slot, target):
+        return pltpu.make_async_remote_copy(
+            src_ref=to_left.at[dest, slot], dst_ref=from_right.at[dest, slot],
+            send_sem=left_send.at[dest, slot], recv_sem=left_recv.at[dest, slot],
+            device_id=(me_d, target, me_s), device_id_type=MESH)
+
+    offset = parts * first_tap(me_t, me_s, per, parts) + me_s - per * me_t
+
+    def spread_copy(slot, other):
+        unit = parts * slot + offset
+        return pltpu.make_async_remote_copy(
+            src_ref=done.at[slot], dst_ref=out_ref.at[unit],
+            send_sem=spread_send.at[other - 1, slot], recv_sem=spread_recv.at[other - 1, slot],
+            device_id=(me_d, me_t, lax.rem(me_s + other, parts)), device_id_type=MESH)
+
+    def step(it, carry):
+        r_slot = it - me_t
+        l_slot = it - (n - 1 - me_t)
+        f_slot = it - n
+        for dist in range(n - 1, 0, -1):
+            dest_r = me_t + dist
+            dest_l = me_t - dist
+
+            @pl.when((dest_r < n) & (r_slot >= 0) & (r_slot < slots))
+            def _():
+                @pl.when(me_t > 0)
+                def _():
+                    right_copy(dest_r, r_slot, me_t).wait_recv()
+                    to_right[dest_r, r_slot] = (
+                        from_left[dest_r, r_slot].astype(jnp.float32) + mine(dest_r, r_slot)
+                    ).astype(jnp.bfloat16)
+
+                @pl.when(me_t == 0)
+                def _():
+                    to_right[dest_r, r_slot] = mine(dest_r, r_slot).astype(jnp.bfloat16)
+
+                right_copy(dest_r, r_slot, me_t + 1).start()
+
+            @pl.when((dest_l >= 0) & (l_slot >= 0) & (l_slot < slots))
+            def _():
+                @pl.when(me_t < n - 1)
+                def _():
+                    left_copy(dest_l, l_slot, me_t).wait_recv()
+                    to_left[dest_l, l_slot] = (
+                        from_right[dest_l, l_slot].astype(jnp.float32) + mine(dest_l, l_slot)
+                    ).astype(jnp.bfloat16)
+
+                @pl.when(me_t == n - 1)
+                def _():
+                    to_left[dest_l, l_slot] = mine(dest_l, l_slot).astype(jnp.bfloat16)
+
+                left_copy(dest_l, l_slot, me_t - 1).start()
+
+        @pl.when(f_slot >= 0)
+        def _():
+            @pl.when(me_t == 0)
+            def _():
+                left_copy(me_t, f_slot, me_t).wait_recv()
+                done[f_slot] = (
+                    mine(me_t, f_slot) + from_right[me_t, f_slot].astype(jnp.float32)
+                ).astype(jnp.bfloat16)
+
+            @pl.when(me_t == n - 1)
+            def _():
+                right_copy(me_t, f_slot, me_t).wait_recv()
+                done[f_slot] = (
+                    mine(me_t, f_slot) + from_left[me_t, f_slot].astype(jnp.float32)
+                ).astype(jnp.bfloat16)
+
+            @pl.when((me_t > 0) & (me_t < n - 1))
+            def _():
+                left_copy(me_t, f_slot, me_t).wait_recv()
+                right_copy(me_t, f_slot, me_t).wait_recv()
+                done[f_slot] = (
+                    mine(me_t, f_slot)
+                    + from_left[me_t, f_slot].astype(jnp.float32)
+                    + from_right[me_t, f_slot].astype(jnp.float32)
+                ).astype(jnp.bfloat16)
+
+            for other in range(1, parts):
+                spread_copy(f_slot, other).start()
+            pltpu.make_async_copy(
+                done.at[f_slot], out_ref.at[parts * f_slot + offset], own_sem.at[f_slot]
+            ).start()
+
+        return carry
+
+    lax.fori_loop(0, n + slots, step, 0)
+
+    def drain(slot, carry):
+        for dist in range(1, n):
+            @pl.when(me_t + dist < n)
+            def _():
+                right_copy(me_t + dist, slot, me_t).wait_send()
+
+            @pl.when(me_t - dist >= 0)
+            def _():
+                left_copy(me_t - dist, slot, me_t).wait_send()
+
+        for other in range(1, parts):
+            spread_copy(slot, other).wait()
+        pltpu.make_async_copy(
+            done.at[slot], out_ref.at[parts * slot + offset], own_sem.at[slot]
+        ).wait()
+        return carry
+
+    lax.fori_loop(0, slots, drain, 0)
+
+
+def reduce_spread(part, n, parts, per, slots):
+    unit, cols = part.shape[1:]
+    block = (n, slots, unit, cols)
+    return pl.pallas_call(
+        functools.partial(reduce_spread_kernel, n, parts, per, slots),
+        out_shape=jax.ShapeDtypeStruct((parts * slots, unit, cols), jnp.bfloat16),
+        in_specs=[pl.BlockSpec(memory_space=pltpu.VMEM)],
+        out_specs=pl.BlockSpec(memory_space=pltpu.VMEM),
+        scratch_shapes=[
+            pltpu.VMEM(block, jnp.bfloat16),
+            pltpu.VMEM(block, jnp.bfloat16),
+            pltpu.VMEM(block, jnp.bfloat16),
+            pltpu.VMEM(block, jnp.bfloat16),
+            pltpu.VMEM((slots, unit, cols), jnp.bfloat16),
+            pltpu.SemaphoreType.DMA((n, slots)),
+            pltpu.SemaphoreType.DMA((n, slots)),
+            pltpu.SemaphoreType.DMA((n, slots)),
+            pltpu.SemaphoreType.DMA((n, slots)),
+            pltpu.SemaphoreType.DMA((parts - 1, slots)),
+            pltpu.SemaphoreType.DMA((parts - 1, slots)),
+            pltpu.SemaphoreType.DMA((slots,)),
+        ],
+        compiler_params=pltpu.CompilerParams(
+            collective_id=0, has_side_effects=True, vmem_limit_bytes=40 * 1024 * 1024
+        ),
+    )(part)
+
+
 def on_device(latents, norm_gain, kernel, conv_bias, out_grad):
     chans = latents.shape[-1]
     half_cols = kernel.shape[1]
@@ -87,15 +268,42 @@
     conv_part = conv_part.reshape(pair_clips, frame_count, row_count, col_count, half_cols)
     conv = lax.all_to_all(conv_part, "dp", split_axis=0, concat_axis=4, tiled=True)
     block_out = (floats + conv + conv_bias).astype(jnp.bfloat16)
-    kernel_local = (
-        lax.dot_general(
-            act_taps,
-            grad_pair.reshape(-1, half_cols),
-            (((0,), (0,)), ((), ())),
-            preferred_element_type=jnp.float32,
+    n_tm, n_space = lax.axis_size("tm"), lax.axis_size("space")
+    units = 27 * n_space
+    split = n_tm > 1 and n_space > 1 and chans % (128 * n_space) == 0 and units % n_tm == 0
+    if split:
+        unit, per = chans // n_space, units // n_tm
+        slots = -(-per // n_space)
+        act_part = lax.all_to_all(joined, "space", split_axis=4, concat_axis=2, tiled=True)
+        act_rows = lax.all_gather(act_part, "dp", axis=0, tiled=True)
+        act_rows = jnp.pad(act_rows, ((0, 0), (0, 0), (1, 1), (1, 1), (0, 0)))
+        grad_rows = lax.all_gather(grad_pair, "space", axis=2, tiled=True)
+        row_taps = tap_columns(act_rows, frame_count, row_count * n_space, col_count, False)
+        part = (
+            lax.dot_general(
+                row_taps,
+                grad_rows.reshape(-1, half_cols),
+                (((0,), (0,)), ((), ())),
+                preferred_element_type=jnp.float32,
+            )
+            * grad_scale
         )
-        * grad_scale
-    )
+        part = jnp.pad(part.reshape(27, unit, half_cols), ((0, 1), (0, 0), (0, 0)))
+        spread = reduce_spread(part, n_tm, n_space, per, slots)
+        kernel_grad = spread.reshape(-1, half_cols)[: per * unit].astype(jnp.float32)
+    else:
+        kernel_local = (
+            lax.dot_general(
+                act_taps,
+                grad_pair.reshape(-1, half_cols),
+                (((0,), (0,)), ((), ())),
+                preferred_element_type=jnp.float32,
+            )
+            * grad_scale
+        )
+        col_part = lax.psum_scatter(kernel_local, "space", scatter_dimension=1, tiled=True)
+        cell_part = lax.psum_scatter(col_part, "tm", scatter_dimension=0, tiled=True)
+        kernel_grad = lax.all_gather(cell_part, "space", axis=1, tiled=True)
     flipped_kernel = jnp.transpose(kernel.reshape(-1, chans, half_cols), (0, 2, 1)).reshape(
         -1, chans
     )
@@ -113,9 +321,6 @@
         normed_grad - normed * jnp.mean(normed_grad * normed, axis=-1, keepdims=True)
     )
     gain_grad, bias_grad = lax.psum((gain_local, bias_local), ("dp", "tm", "space"))
-    col_part = lax.psum_scatter(kernel_local, "space", scatter_dimension=1, tiled=True)
-    cell_part = lax.psum_scatter(col_part, "tm", scatter_dimension=0, tiled=True)
-    kernel_grad = lax.all_gather(cell_part, "space", axis=1, tiled=True)
     return (block_out, latent_grad.astype(jnp.bfloat16), kernel_grad, gain_grad, bias_grad)
 
 

time: 406 us -> 268 us (0.66)
  waiting for transfers between devices: 261 us -> 30.5 us
  Pallas kernels: 0 us -> 43.9 us
  local copies, waits for them, and re-layouts: 33 us -> 61.3 us
  blocking collectives: 49.4 us -> 70 us
  matrix products: 25.4 us -> 20.2 us
    reduce_scatter x2 -> x0, waiting for transfers between devices: 203 us -> none  [the longest x1 135 us: on_device(): lax.psum_scatter(kernel_local, 'space', scatter_dimension=1, tiled=True)]
    pallas_call x0 -> x1, Pallas kernels: none -> 43.9 us  [reduce_spread(): pl.pallas_call(functools.partial(reduce_spread_kernel, n, parts, per, slo...]
    unnamed x69 -> x100, local copies, waits for them, and re-layouts: 22 us -> 45.6 us
    all_to_all x0 -> x1, blocking collectives: none -> 17.2 us  [on_device(): lax.all_to_all(joined, 'space', split_axis=4, concat_axis=2, tiled=True)]
    ppermute x2, waiting for transfers between devices: 12.7 us -> 0.01 us  [padded(): lax.ppermute(lax.slice_in_dim(block, 0, width, axis=dim), axis, backward)]
    all_gather x1, waiting for transfers between devices: 12.3 us -> 0.01 us  [on_device(): act_pair = lax.all_gather(act_ext, 'dp', axis=0, tiled=True)]
    dot_general x1, matrix products: 10.5 us -> 4.71 us  [on_device(): conv_part = jnp.dot(act_taps, kernel, preferred_element_type=jnp.float32)]
    ppermute x2, waiting for transfers between devices: 5.25 us -> 0.01 us  [padded(): lax.ppermute(lax.slice_in_dim(block, block.shape[dim] - width, None, axis...]
  transfers between devices with their start and end apart: 11 -> 10, of which waited for: 9 -> 3; matrix products, arithmetic and copies ran while one was open for 5% -> 22% of each run, Pallas kernels for 0% -> 16%
where the time goes in v1:
time: 268 us; the launch traced here: 267 us
  blocking collectives  70 us (26%)
  local copies, waits for them, and re-layouts  61.3 us (23%)
  Pallas kernels  43.9 us (16%)
  waiting for transfers between devices  30.5 us (11%)
  matrix products  20.2 us (8%)
  starting transfers between devices  16.8 us (6%)
  between operations  14.5 us (5%)
  other arithmetic  9.48 us (4%)
    unnamed x100, local copies, waits for them, and re-layouts  45.6 us
    psum x1, blocking collectives, on_device(): lax.psum((gain_local, bias_local), ('dp', 'tm', 'space'))  44.3 us
    pallas_call x1, Pallas kernels, reduce_spread(): pl.pallas_call(functools.partial(reduce_spread_kernel, n, parts, per, slo...  43.9 us
    ppermute x2, waiting for transfers between devices, shifted(): return lax.ppermute(block, axis, route)  19 us
    all_to_all x1, blocking collectives, on_device(): lax.all_to_all(joined, 'space', split_axis=4, concat_axis=2, tiled=True)  17.2 us
    reduce_scatter x1, waiting for transfers between devices, on_device(): lax.psum_scatter(partial_grad, 'dp', scatter_dimension=0, tiled=True)  10.7 us
    transpose x1, local copies, waits for them, and re-layouts, on_device(): jnp.transpose(kernel.reshape(-1, chans, half_cols), (0, 2, 1))  10.3 us
    dot_general x1, matrix products, on_device(): lax.dot_general(row_taps, grad_rows.reshape(-1, half_cols), (((0,), (0,))...  9.67 us
  transfers between devices with their start and end apart: 10, of which 3 were waited for; matrix products, arithmetic and copies ran while one was open for 22% of the time, Pallas kernels for 16%

profile of v1, /device:TPU:0, one launch (start us, length us, event | category | flops | bytes accessed | tf_op | source)
XLA Modules:
  0.0 266.6 jit_solution(10226774254445150367)
XLA Ops:
  8.5 4.2 %all_to_all.54 = bf16[1,2,2,80,512]{3,2,1,0,4:T(2,128)(2,1)S(1)} all-to-all(bf16[1,2,2,80,512]{3,2,1,0,4:T(2,128)(2,1)S(1)} %copy.24), channel_id=1, replica_groups=mesh['dp'=2,'tm'=4,'space'=4] {'dp'}, dimensions={4} | all-to-all | bytes 655360 | tf_op jit(solution)/shard_map/all_to_all | solution.py:257
  14.3 11.6 %collective-permute-done.3 = bf16[2,2,2,80,256]{4,3,2,1,0:T(8,128)(2,1)S(1)} collective-permute-done((bf16[2,2,2,80,256]{4,3,2,1,0:T(8,128)(2,1)S(1)}, bf16[2,2,2,80,256]{4,3,2,1,0:T(8,128)(2,1)S(1)}, u32[]{:S(2)}, u32[]{:S(2)}) %collective-permute-start.3) | collective-permute-done | bytes 327712 | tf_op jit(solution)/shard_map/ppermute | solution.py:14
  27.3 4.6 %collective-permute-start.4 = (bf16[2,4,1,80,256]{4,3,2,1,0:T(8,128)(2,1)S(1)}, bf16[2,4,1,80,256]{4,3,2,1,0:T(8,128)(2,1)S(1)}, u32[]{:S(2)}, u32[]{:S(2)}) collective-permute-start(bf16[2,4,1,80,256]{4,3,2,1,0:T(8,128)(2,1)S(1)} %get-tuple-element.11), channel_id=1, source_target_pairs={{0,1},{1,2},{2,3},{4,5},{5,6},{6,7},{8,9},{9,10},{10,11},{12,13},{... | collective-permute-start | bytes 983048 | tf_op jit(solution)/shard_map/ppermute | solution.py:22
  31.9 10.3 %copy.27 = bf16[27,256,512]{2,1,0:T(8,128)(2,1)} copy(bf16[27,256,512]{1,2,0:T(8,128)(2,1)} %bitcast.50) | data formatting | bytes 14155776 | tf_op jit(solution)/shard_map/transpose | solution.py:307
  46.5 5.8 %fusion.58 = f32[2,2,2,80,512]{4,3,2,1,0:T(8,128)} fusion(bf16[2,2,2,80,6912]{4,3,2,1,0:T(8,128)(2,1)S(1)} %slice_dynamic-update-slice_fusion.30, bf16[6912,512,1,1,1]{1,0,4,3,2:T(8,128)(2,1)S(1)} %bitcast.55), kind=kOutput, calls=%fused_computation.166 | convolution fusion | flops 4529848320 | bytes 17235968 | tf_op jit(solution)/shard_map/dot_general | solution.py:311
  52.5 10.7 %reduce-scatter.2.cloned.1.call-done = f32[1,2,2,80,512]{4,3,2,1,0:T(8,128)} async-done(((f32[2,2,2,80,512]{4,3,2,1,0:T(8,128)}), f32[1,2,2,80,512]{4,3,2,1,0:T(8,128)}) %reduce-scatter.2.cloned.1.call-update) | async-done | bytes 655376 | tf_op jit(solution)/shard_map/reduce_scatter | solution.py:313
  63.2 1.6 fusion.25
  64.8 2.4 fusion.15
  67.2 3.7 %collective-permute-start = (bf16[1,2,2,80,512]{4,3,2,1,0:T(8,128)(2,1)S(1)}, bf16[1,2,2,80,512]{4,3,2,1,0:T(8,128)(2,1)S(1)}, u32[]{:S(2)}, u32[]{:S(2)}) collective-permute-start(bf16[1,2,2,80,512]{4,3,2,1,0:T(8,128)(2,1)S(1)} %get-tuple-element.16), channel_id=1, source_target_pairs={{0,4},{4,8},{8,12},{1,5},{5,9},{9,13},{2,6},{6,10},{10,14},{3,7},{... | collective-permute-start | bytes 983048 | tf_op jit(solution)/shard_map/ppermute | solution.py:14
  70.8 7.4 %collective-permute-done = bf16[1,2,2,80,512]{4,3,2,1,0:T(8,128)(2,1)S(1)} collective-permute-done((bf16[1,2,2,80,512]{4,3,2,1,0:T(8,128)(2,1)S(1)}, bf16[1,2,2,80,512]{4,3,2,1,0:T(8,128)(2,1)S(1)}, u32[]{:S(2)}, u32[]{:S(2)}) %collective-permute-start) | collective-permute-done | bytes 327712 | tf_op jit(solution)/shard_map/ppermute | solution.py:14
  79.2 17.2 %all_to_all.55 = bf16[1,4,2,80,512]{3,2,1,0,4:T(2,128)(2,1)S(1)} all-to-all(bf16[1,4,2,80,512]{3,2,1,0,4:T(2,128)(2,1)S(1)} %copy.28), channel_id=1, replica_groups=mesh['dp'=2,'tm'=4,'space'=4] {'space'}, dimensions={4} | all-to-all | bytes 1310720 | tf_op jit(solution)/shard_map/all_to_all | solution.py:277
  96.4 2.3 copy.29
  100.9 4.6 %collective-permute-start.1 = (bf16[1,4,1,80,512]{4,3,2,1,0:T(8,128)(2,1)S(1)}, bf16[1,4,1,80,512]{4,3,2,1,0:T(8,128)(2,1)S(1)}, u32[]{:S(2)}, u32[]{:S(2)}) collective-permute-start(bf16[1,4,1,80,512]{4,3,2,1,0:T(8,128)(2,1)S(1)} %get-tuple-element.13), channel_id=1, source_target_pairs={{0,1},{1,2},{2,3},{4,5},{5,6},{6,7},{8,9},{9,10},{10,11},{12,13},{... | collective-permute-start | bytes 983048 | tf_op jit(solution)/shard_map/ppermute | solution.py:22
  105.5 44.3 %all-reduce.4 = (f32[512]{0:T(512)}, f32[512]{0:T(512)}) all-reduce(f32[512]{0:T(512)S(1)} %broadcast_multiply_fusion.1, f32[512]{0:T(512)S(1)} %broadcast_multiply_fusion), channel_id=1, replica_groups=mesh['dp'=2,'tm'=4,'space'=4] {'dp','tm','space'}, use_global_device_ids=true, to_apply=%region_4.5 | all-reduce | flops 1024 | bytes 8192 | tf_op jit(solution)/shard_map/psum | solution.py:323
  151.1 2.2 fusion.29
  153.3 2.0 fusion.30
  155.3 2.1 fusion.31
  157.4 2.2 fusion.32
  159.6 2.1 slice_dynamic-update-slice_fusion.2
  184.8 9.7 %fusion.2 = f32[3456,256]{1,0:T(8,128)S(1)} fusion(bf16[2,2,8,80,3456]{4,3,2,1,0:T(8,128)(2,1)} %fusion.52, bf16[2,1,2,8,80,256]{5,4,3,2,0,1:T(8,128)(2,1)} %all-gather.9.cloned.1.call-done), kind=kOutput, calls=%fused_computation.3 | convolution fusion | flops 4530733056 | bytes 22544384 | tf_op jit(solution)/shard_map/dot_general | solution.py:283
  194.9 43.9 %shard_map.92 = bf16[28,128,256]{2,1,0:T(8,128)(2,1)S(1)} custom-call(f32[28,128,256]{2,1,0:T(8,128)S(1)} %pad.19.part_ref), custom_call_target="tpu_custom_call" | custom-call | tf_op jit(solution)/shard_map/pallas_call | solution.py:208
  238.9 2.2 bitcast_convert_fusion
  250.2 4.7 %fusion = f32[2,2,2,80,256]{4,3,2,1,0:T(8,128)S(1)} fusion(bf16[2,2,2,80,13824]{4,3,2,1,0:T(8,128)(2,1)S(1)} %slice_dynamic-update-slice_fusion.12, bf16[13824,256]{1,0:T(8,128)(2,1)S(1)} %bitcast.52), kind=kOutput, calls=%fused_computation | convolution fusion | flops 4529848320 | bytes 25427968 | tf_op jit(solution)/shard_map/dot_general | solution.py:267
  254.9 4.3 %all_to_all.56 = f32[2,2,2,80,256]{4,3,2,1,0:T(8,128)S(1)} all-to-all(f32[2,2,2,80,256]{4,3,2,1,0:T(8,128)S(1)} %fusion), channel_id=1, replica_groups=mesh['dp'=2,'tm'=4,'space'=4] {'dp'}, dimensions={0} | all-to-all | bytes 1310720 | tf_op jit(solution)/shard_map/all_to_all | solution.py:269
  (136 shorter events, 46.2 us)
Async XLA Ops:
  7.2 56.0 %reduce-scatter.2.cloned.1.call-start = ((), (), s32[]{:S(2)}) async-start(), calls=%async_computation.5 | async-start | bytes 1966080 | tf_op jit(solution)/shard_map/reduce_scatter | solution.py:313
  13.0 31.3 %copy-start.2 = (bf16[1,2,2,80,2,256]{5,3,2,1,4,0:T(8,128)(2,1)}, bf16[1,2,2,80,2,256]{5,3,2,1,4,0:T(8,128)(2,1)S(1)}, u32[]{:S(2)}) copy-start(bf16[1,2,2,80,2,256]{5,3,2,1,4,0:T(8,128)(2,1)S(1)} %copy.26) | copy-start | bytes 983044
  13.0 12.9 %collective-permute-start.3 = (bf16[2,2,2,80,256]{4,3,2,1,0:T(8,128)(2,1)S(1)}, bf16[2,2,2,80,256]{4,3,2,1,0:T(8,128)(2,1)S(1)}, u32[]{:S(2)}, u32[]{:S(2)}) collective-permute-start(bf16[2,2,2,80,256]{4,3,2,1,0:T(8,128)(2,1)S(1)} %bitcast.44), channel_id=1, source_target_pairs={{4,0},{8,4},{12,8},{5,1},{9,5},{13,9},{6,2},{10,6},{14,10},{7,3},{... | collective-permute-start | bytes 983048 | tf_op jit(solution)/shard_map/ppermute | solution.py:14
  26.0 16.2 %collective-permute-start.5 = (bf16[2,4,1,80,256]{4,3,2,1,0:T(8,128)(2,1)S(1)}, bf16[2,4,1,80,256]{4,3,2,1,0:T(8,128)(2,1)S(1)}, u32[]{:S(2)}, u32[]{:S(2)}) collective-permute-start(bf16[2,4,1,80,256]{4,3,2,1,0:T(8,128)(2,1)S(1)} %get-tuple-element.12), channel_id=1, source_target_pairs={{1,0},{2,1},{3,2},{5,4},{6,5},{7,6},{9,8},{10,9},{11,10},{13,12},{... | collective-permute-start | bytes 983048 | tf_op jit(solution)/shard_map/ppermute | solution.py:25
  27.3 14.9 %collective-permute-start.4 = (bf16[2,4,1,80,256]{4,3,2,1,0:T(8,128)(2,1)S(1)}, bf16[2,4,1,80,256]{4,3,2,1,0:T(8,128)(2,1)S(1)}, u32[]{:S(2)}, u32[]{:S(2)}) collective-permute-start(bf16[2,4,1,80,256]{4,3,2,1,0:T(8,128)(2,1)S(1)} %get-tuple-element.11), channel_id=1, source_target_pairs={{0,1},{1,2},{2,3},{4,5},{5,6},{6,7},{8,9},{9,10},{10,11},{12,13},{... | collective-permute-start | bytes 983048 | tf_op jit(solution)/shard_map/ppermute | solution.py:22
  43.2 2.2 slice-start.2
  43.8 2.6 slice-start.3
  46.5 5.9 %copy-start.3 = (bf16[1,2,2,80,512]{4,3,2,1,0:T(8,128)(2,1)S(1)}, bf16[1,2,2,80,512]{4,3,2,1,0:T(8,128)(2,1)}, u32[]{:S(2)}) copy-start(bf16[1,2,2,80,512]{4,3,2,1,0:T(8,128)(2,1)} %param.5) | copy-start | bytes 983044
  46.5 16.7 %copy-start.5 = (f32[512]{0:T(512)S(1)}, f32[512]{0:T(512)}, u32[]{:S(2)}) copy-start(f32[512]{0:T(512)} %param.6) | copy-start | bytes 6148
  46.5 18.4 %copy-start.4 = (bf16[1,2,2,80,512]{4,3,2,1,0:T(8,128)(2,1)S(1)}, bf16[1,2,2,80,512]{4,3,2,1,0:T(8,128)(2,1)}, u32[]{:S(2)}) copy-start(bf16[1,2,2,80,512]{4,3,2,1,0:T(8,128)(2,1)} %param.9) | copy-start | bytes 983044
  52.3 98.8 %all-gather.7.cloned.1.call-start = ((), (), s32[]{:S(2)}) async-start(), calls=%async_computation.6 | async-start | bytes 1966080 | tf_op jit(solution)/shard_map/all_gather | solution.py:278
  67.2 11.1 %collective-permute-start = (bf16[1,2,2,80,512]{4,3,2,1,0:T(8,128)(2,1)S(1)}, bf16[1,2,2,80,512]{4,3,2,1,0:T(8,128)(2,1)S(1)}, u32[]{:S(2)}, u32[]{:S(2)}) collective-permute-start(bf16[1,2,2,80,512]{4,3,2,1,0:T(8,128)(2,1)S(1)} %get-tuple-element.16), channel_id=1, source_target_pairs={{0,4},{4,8},{8,12},{1,5},{5,9},{9,13},{2,6},{6,10},{10,14},{3,7},{... | collective-permute-start | bytes 983048 | tf_op jit(solution)/shard_map/ppermute | solution.py:14
  98.7 86.1 %all-gather.9.cloned.1.call-start = ((), (), s32[]{:S(2)}) async-start(), calls=%async_computation.7 | async-start | bytes 1638400 | tf_op jit(solution)/shard_map/all_gather | solution.py:280
  99.5 141.6 %all-gather.5.cloned.1.call-start = ((), (), s32[]{:S(2)}) async-start(), calls=%async_computation.4 | async-start | bytes 3932160 | tf_op jit(solution)/shard_map/all_gather | solution.py:264
  99.6 50.2 %collective-permute-start.2 = (bf16[1,4,1,80,512]{4,3,2,1,0:T(8,128)(2,1)S(1)}, bf16[1,4,1,80,512]{4,3,2,1,0:T(8,128)(2,1)S(1)}, u32[]{:S(2)}, u32[]{:S(2)}) collective-permute-start(bf16[1,4,1,80,512]{4,3,2,1,0:T(8,128)(2,1)S(1)} %get-tuple-element.14), channel_id=1, source_target_pairs={{1,0},{2,1},{3,2},{5,4},{6,5},{7,6},{9,8},{10,9},{11,10},{13,12},{... | collective-permute-start | bytes 983048 | tf_op jit(solution)/shard_map/ppermute | solution.py:25
  100.9 48.9 %collective-permute-start.1 = (bf16[1,4,1,80,512]{4,3,2,1,0:T(8,128)(2,1)S(1)}, bf16[1,4,1,80,512]{4,3,2,1,0:T(8,128)(2,1)S(1)}, u32[]{:S(2)}, u32[]{:S(2)}) collective-permute-start(bf16[1,4,1,80,512]{4,3,2,1,0:T(8,128)(2,1)S(1)} %get-tuple-element.13), channel_id=1, source_target_pairs={{0,1},{1,2},{2,3},{4,5},{5,6},{6,7},{8,9},{9,10},{10,11},{12,13},{... | collective-permute-start | bytes 983048 | tf_op jit(solution)/shard_map/ppermute | solution.py:22
  151.1 10.7 %copy-start.1 = (bf16[2,4,8,80,128]{4,3,2,1,0:T(8,128)(2,1)S(1)}, bf16[2,4,8,80,128]{4,3,2,1,0:T(8,128)(2,1)}, u32[]{:S(2)}) copy-start(bf16[2,4,8,80,128]{4,3,2,1,0:T(8,128)(2,1)} %all-gather.7.cloned.1.call-done) | copy-start | bytes 3932164
  241.1 3.8 %copy-start = (bf16[2,4,4,80,512]{4,3,2,1,0:T(8,128)(2,1)S(1)}, bf16[2,4,4,80,512]{4,3,2,1,0:T(8,128)(2,1)}, u32[]{:S(2)}) copy-start(bf16[2,4,4,80,512]{4,3,2,1,0:T(8,128)(2,1)} %all-gather.5.cloned.1.call-done) | copy-start | bytes 7864324
  247.0 2.2 slice-start
  247.4 2.8 %slice-start.1 = ((s8[7077888]{0:T(1024)(128)(4,1)}), s8[2883584]{0:T(1024)(128)(4,1)S(1)}, s32[]{:S(2)}) async-start(s8[7077888]{0:T(1024)(128)(4,1)} %bitcast.51), calls=%async_computation.9 | async-start | bytes 5767168
  250.2 9.1 %copy-start.6 = (f32[512]{0:T(512)S(1)}, f32[512]{0:T(512)}, u32[]{:S(2)}) copy-start(f32[512]{0:T(512)} %param.8) | copy-start | bytes 6148
Sparse Core Ops, SparseCore 0:
  52.4 10.7 reduce-scatter.1
  98.8 9.8 all-gather.6
  111.3 30.2 all-gather.8
  151.2 12.0 all-gather.4

commit v2 on v1

--- a/solution.py
+++ b/solution.py
@@ -1,4 +1,5 @@
 import functools
+import math
 
 import jax
 import jax.numpy as jnp
@@ -60,29 +61,74 @@
     return (per * owner - quarter + parts - 1) // parts
 
 
-def reduce_spread_kernel(
-    n, parts, per, slots, part_ref, out_ref, from_left, from_right, to_right, to_left, done,
-    right_send, right_recv, left_send, left_recv, spread_send, spread_recv, own_sem,
-):
+def greet(n, parts):
     me_d, me_t, me_s = lax.axis_index("dp"), lax.axis_index("tm"), lax.axis_index("space")
     barrier = pltpu.get_barrier_semaphore()
 
-    def signal(t, s):
-        pl.semaphore_signal(barrier, inc=1, device_id=(me_d, t, s), device_id_type=MESH)
+    def signal(d, t, s):
+        pl.semaphore_signal(barrier, inc=1, device_id=(d, t, s), device_id_type=MESH)
 
     for other in range(1, parts):
-        signal(me_t, lax.rem(me_s + other, parts))
-
-    @pl.when(me_t > 0)
-    def _():
-        signal(me_t - 1, me_s)
-
-    @pl.when(me_t < n - 1)
-    def _():
-        signal(me_t + 1, me_s)
-
-    ends = jnp.where(me_t > 0, 1, 0) + jnp.where(me_t < n - 1, 1, 0)
-    pl.semaphore_wait(barrier, parts - 1 + ends)
+        signal(me_d, me_t, lax.rem(me_s + other, parts))
+    for other in range(1, n):
+        signal(me_d, lax.rem(me_t + other, n), me_s)
+    signal(1 - me_d, me_t, me_s)
+    pl.semaphore_wait(barrier, parts + n - 1)
+    return me_d, me_t, me_s
+
+
+def reduce_spread_kernel(
+    n, parts, per, slots, grad_scale, act_ref, cot_ref, vec_ref, out_ref, vec_out,
+    part_ref, from_left, from_right, to_right, to_left, done, vec_plane, vec_line, vec_pair,
+    right_send, right_recv, left_send, left_recv, spread_send, spread_recv, own_sem,
+    plane_send, plane_recv, line_send, line_recv, pair_send, pair_recv,
+):
+    me_d, me_t, me_s = greet(n, parts)
+    half = out_ref.shape[-1]
+    frames, rows = act_ref.shape[1] // 2, act_ref.shape[2] - 2
+
+    def plane_copy(other):
+        return pltpu.make_async_remote_copy(
+            src_ref=vec_ref, dst_ref=vec_plane.at[me_s],
+            send_sem=plane_send.at[other - 1], recv_sem=plane_recv.at[other - 1],
+            device_id=(me_d, me_t, lax.rem(me_s + other, parts)), device_id_type=MESH)
+
+    def line_copy(other):
+        return pltpu.make_async_remote_copy(
+            src_ref=vec_line.at[me_t], dst_ref=vec_line.at[me_t],
+            send_sem=line_send.at[other - 1], recv_sem=line_recv.at[other - 1],
+            device_id=(me_d, lax.rem(me_t + other, n), me_s), device_id_type=MESH)
+
+    pair_copy = pltpu.make_async_remote_copy(
+        src_ref=vec_pair.at[0], dst_ref=vec_pair.at[1],
+        send_sem=pair_send, recv_sem=pair_recv,
+        device_id=(1 - me_d, me_t, me_s), device_id_type=MESH)
+
+    for other in range(1, parts):
+        plane_copy(other).start()
+    vec_plane[me_s] = vec_ref[...]
+
+    for tap_t in range(3):
+        for tap_h in range(3):
+            total = None
+            for clip in range(2):
+                window = act_ref[clip, tap_t : tap_t + frames, tap_h : tap_h + rows]
+                term = lax.dot_general(
+                    window.reshape(-1, window.shape[-1]), cot_ref[clip],
+                    (((0,), (0,)), ((), ())), preferred_element_type=jnp.float32)
+                total = term if total is None else total + term
+            total = total * grad_scale
+            for tap_w in range(3):
+                part_ref[9 * tap_t + 3 * tap_h + tap_w] = total[
+                    :, tap_w * half : (tap_w + 1) * half
+                ]
+    part_ref[27] = jnp.zeros_like(part_ref[27])
+
+    for other in range(1, parts):
+        plane_copy(other).wait()
+    vec_line[me_t] = functools.reduce(lambda a, b: a + b, [vec_plane[i] for i in range(parts)])
+    for other in range(1, n):
+        line_copy(other).start()
 
     def mine(dest, slot):
         return part_ref[first_tap(dest, me_s, per, parts) + slot]
@@ -182,6 +228,11 @@
 
     lax.fori_loop(0, n + slots, step, 0)
 
+    for other in range(1, n):
+        line_copy(other).wait()
+    vec_pair[0] = functools.reduce(lambda a, b: a + b, [vec_line[i] for i in range(n)])
+    pair_copy.start()
+
     def drain(slot, carry):
         for dist in range(1, n):
             @pl.when(me_t + dist < n)
@@ -200,37 +251,351 @@
         return carry
 
     lax.fori_loop(0, slots, drain, 0)
-
-
-def reduce_spread(part, n, parts, per, slots):
-    unit, cols = part.shape[1:]
+    pair_copy.wait()
+    vec_out[...] = vec_pair[0] + vec_pair[1]
+
+
+def reduce_spread(act_rows, cot_rows, vec, n, parts, per, slots, grad_scale):
+    unit, cols = act_rows.shape[-1], cot_rows.shape[-1] // 3
     block = (n, slots, unit, cols)
+    dma = pltpu.SemaphoreType.DMA
+    vmem = pl.BlockSpec(memory_space=pltpu.VMEM)
     return pl.pallas_call(
-        functools.partial(reduce_spread_kernel, n, parts, per, slots),
-        out_shape=jax.ShapeDtypeStruct((parts * slots, unit, cols), jnp.bfloat16),
-        in_specs=[pl.BlockSpec(memory_space=pltpu.VMEM)],
-        out_specs=pl.BlockSpec(memory_space=pltpu.VMEM),
-        scratch_shapes=[
-            pltpu.VMEM(block, jnp.bfloat16),
-            pltpu.VMEM(block, jnp.bfloat16),
-            pltpu.VMEM(block, jnp.bfloat16),
-            pltpu.VMEM(block, jnp.bfloat16),
+        functools.partial(reduce_spread_kernel, n, parts, per, slots, grad_scale),
+        out_shape=(
+            jax.ShapeDtypeStruct((parts * slots, unit, cols), jnp.bfloat16),
+            jax.ShapeDtypeStruct(vec.shape, jnp.float32),
+        ),
+        in_specs=[vmem] * 3,
+        out_specs=(vmem, vmem),
+        scratch_shapes=[pltpu.VMEM((28, unit, cols), jnp.float32)]
+        + [pltpu.VMEM(block, jnp.bfloat16)] * 4
+        + [
             pltpu.VMEM((slots, unit, cols), jnp.bfloat16),
-            pltpu.SemaphoreType.DMA((n, slots)),
-            pltpu.SemaphoreType.DMA((n, slots)),
-            pltpu.SemaphoreType.DMA((n, slots)),
-            pltpu.SemaphoreType.DMA((n, slots)),
-            pltpu.SemaphoreType.DMA((parts - 1, slots)),
-            pltpu.SemaphoreType.DMA((parts - 1, slots)),
-            pltpu.SemaphoreType.DMA((slots,)),
-        ],
+            pltpu.VMEM((parts,) + vec.shape, jnp.float32),
+            pltpu.VMEM((n,) + vec.shape, jnp.float32),
+            pltpu.VMEM((2,) + vec.shape, jnp.float32),
+        ]
+        + [dma((n, slots))] * 4
+        + [dma((parts - 1, slots))] * 2
+        + [dma((slots,))]
+        + [dma((parts - 1,))] * 2
+        + [dma((n - 1,))] * 2
+        + [dma, dma],
         compiler_params=pltpu.CompilerParams(
-            collective_id=0, has_side_effects=True, vmem_limit_bytes=40 * 1024 * 1024
+            collective_id=0, has_side_effects=True, vmem_limit_bytes=48 * 1024 * 1024
         ),
-    )(part)
+    )(act_rows, cot_rows, vec)
+
+
+def exchange_kernel(n, parts, act_ref, grad_ref, af, aq, gr, gn, send, recv, local):
+    me_d, me_t, me_s = greet(n, parts)
+    frames, rows, _, chans = act_ref.shape
+    half, quarter = gr.shape[-1], aq.shape[-1]
+    before, now = pl.ds(0, frames), pl.ds(frames, frames)
+    inner = pl.ds(1, rows)
+    own = pl.ds(1 + me_s * rows, rows)
+    last = 1 + parts * rows
+
+    def channels(index, size):
+        return pl.ds(pl.multiple_of(index * size, size), size)
+
+    def remote(i, src, dst, d, t, s):
+        return pltpu.make_async_remote_copy(
+            src_ref=src, dst_ref=dst, send_sem=send.at[i], recv_sem=recv.at[i],
+            device_id=(d, t, s), device_id_type=MESH)
+
+    partner = (1 - me_d, me_t, me_s)
+    peers = [lax.rem(me_s + other, parts) for other in range(1, parts)]
+
+    first = 0
+    to_partner = remote(
+        first, grad_ref.at[:, :, :, channels(1 - me_d, half)], gr.at[me_d, :, own], *partner)
+    to_partner.start()
+    later = remote(1, act_ref, af.at[me_d, before, inner], me_d, me_t + 1, me_s)
+
+    @pl.when(me_t < n - 1)
+    def _():
+        later.start()
+
+    def quarter_copy(i, peer, source, when):
+        return remote(
+            i, source.at[:, :, :, channels(peer, quarter)], aq.at[me_d, when, own],
+            me_d, me_t, peer)
+
+    def edge_down(i, source, row, dst):
+        return remote(i, source.at[:, row], dst, me_d, me_t, me_s + 1)
+
+    def edge_up(i, source, row, dst):
+        return remote(i, source.at[:, row], dst, me_d, me_t, me_s - 1)
+
+    base = 2
+    quarters_now = [quarter_copy(base + i, peer, act_ref, now) for i, peer in enumerate(peers)]
+    base += parts - 1
+    down_now = edge_down(base, act_ref, rows - 1, af.at[me_d, now, 0])
+    up_now = edge_up(base + 1, act_ref, 0, af.at[me_d, now, rows + 1])
+    base += 2
+    own_rows = gr.at[:, :, own]
+    gather = [remote(base + i, own_rows, own_rows, me_d, me_t, peer) for i, peer in enumerate(peers)]
+    base += parts - 1
+    sooner = remote(base, own_rows, gn.at[:, :, inner], me_d, me_t - 1, me_s)
+    base += 1
+    past = af.at[me_d, before, inner]
+    quarters_before = [quarter_copy(base + i, peer, past, before) for i, peer in enumerate(peers)]
+    base += parts - 1
+    down_before = edge_down(base, past, rows - 1, af.at[me_d, before, 0])
+    up_before = edge_up(base + 1, past, 0, af.at[me_d, before, rows + 1])
+    base += 2
+    down_next = edge_down(base, gn.at[0], rows, gn.at[0, :, 0])
+    down_next2 = edge_down(base + 1, gn.at[1], rows, gn.at[1, :, 0])
+    up_next = edge_up(base + 2, gn.at[0], 1, gn.at[0, :, rows + 1])
+    up_next2 = edge_up(base + 3, gn.at[1], 1, gn.at[1, :, rows + 1])
+    base += 4
+    forward = [
+        remote(base + i, ref.at[me_d, when], ref.at[me_d, when], *partner)
+        for i, (ref, when) in enumerate(((aq, now), (af, now), (aq, before), (af, before)))
+    ]
+
+    keep = [
+        pltpu.make_async_copy(
+            grad_ref.at[:, :, :, channels(me_d, half)], gr.at[me_d, :, own], local.at[0]),
+        pltpu.make_async_copy(
+            act_ref.at[:, :, :, channels(me_s, quarter)], aq.at[me_d, now, own], local.at[1]),
+        pltpu.make_async_copy(act_ref, af.at[me_d, now, inner], local.at[2]),
+    ]
+    keep_before = pltpu.make_async_copy(
+        past.at[:, :, :, channels(me_s, quarter)], aq.at[me_d, before, own], local.at[3])
+
+    below, above = me_s < parts - 1, me_s > 0
+    for copy in keep:
+        copy.start()
+    for copy in quarters_now:
+        copy.start()
+
+    def start_if(condition, *copies):
+        @pl.when(condition)
+        def _():
+            for copy in copies:
+                copy.start()
+
+    start_if(below, down_now)
+    start_if(above, up_now)
+
+    def clear(ref, *index):
+        ref[index] = jnp.zeros(ref.at[index].shape, ref.dtype)
+
+    everything = slice(None)
+    for row in (0, last):
+        clear(gr, everything, everything, row)
+        clear(aq, me_d, everything, row)
+
+    @pl.when(me_s == 0)
+    def _():
+        clear(af, me_d, everything, 0)
+        clear(gn, everything, everything, 0)
+
+    @pl.when(me_s == parts - 1)
+    def _():
+        clear(af, me_d, everything, rows + 1)
+        clear(gn, everything, everything, rows + 1)
+
+    to_partner.wait_recv()
+    keep[0].wait()
+    start_if(me_t > 0, sooner)
+    for copy in gather:
+        copy.start()
+
+    @pl.when(me_t > 0)
+    def _():
+        later.wait_recv()
+        keep_before.start()
+        for copy in quarters_before:
+            copy.start()
+        start_if(below, down_before)
+        start_if(above, up_before)
+
+    @pl.when(me_t == 0)
+    def _():
+        clear(aq, me_d, before, pl.ds(1, parts * rows))
+        clear(af, me_d, before, inner)
+
+        @pl.when(above)
+        def _():
+            clear(af, me_d, before, 0)
+
+        @pl.when(below)
+        def _():
+            clear(af, me_d, before, rows + 1)
+
+    keep[1].wait()
+    keep[2].wait()
+    for copy in quarters_now:
+        copy.wait_recv()
+
+    def received(condition, *copies):
+        @pl.when(condition)
+        def _():
+            for copy in copies:
+                copy.wait_recv()
+
+    received(above, down_now)
+    received(below, up_now)
+    forward[0].start()
+    forward[1].start()
+
+    @pl.when(me_t < n - 1)
+    def _():
+        sooner.wait_recv()
+        start_if(below, down_next, down_next2)
+        start_if(above, up_next, up_next2)
+
+    @pl.when(me_t == n - 1)
+    def _():
+        clear(gn, everything, everything, inner)
+
+        @pl.when(above)
+        def _():
+            clear(gn, everything, everything, 0)
+
+        @pl.when(below)
+        def _():
+            clear(gn, everything, everything, rows + 1)
+
+    @pl.when(me_t > 0)
+    def _():
+        keep_before.wait()
+        for copy in quarters_before:
+            copy.wait_recv()
+        received(above, down_before)
+        received(below, up_before)
+
+    forward[2].start()
+    forward[3].start()
+
+    @pl.when(me_t < n - 1)
+    def _():
+        received(above, down_next, down_next2)
+        received(below, up_next, up_next2)
+
+    for copy in gather:
+        copy.wait_recv()
+    for copy in forward:
+        copy.wait_recv()
+
+    def sent(condition, *copies):
+        @pl.when(condition)
+        def _():
+            for copy in copies:
+                copy.wait_send()
+
+    for copy in [to_partner] + quarters_now + gather + forward:
+        copy.wait_send()
+    sent(below, down_now)
+    sent(above, up_now)
+    sent(me_t < n - 1, later)
+    sent(me_t > 0, sooner, *quarters_before)
+    sent((me_t > 0) & below, down_before)
+    sent((me_t > 0) & above, up_before)
+    sent((me_t < n - 1) & below, down_next, down_next2)
+    sent((me_t < n - 1) & above, up_next, up_next2)
+
+
+def exchange(act, grad, n, parts):
+    frames, rows, cols, chans = act.shape
+    half, quarter = chans // 2, chans // parts
+    messages = 4 * (parts - 1) + 15
+    dma = pltpu.SemaphoreType.DMA
+    vmem = pl.BlockSpec(memory_space=pltpu.VMEM)
+    return pl.pallas_call(
+        functools.partial(exchange_kernel, n, parts),
+        out_shape=(
+            jax.ShapeDtypeStruct((2, 2 * frames, rows + 2, cols, chans), jnp.bfloat16),
+            jax.ShapeDtypeStruct((2, 2 * frames, parts * rows + 2, cols, quarter), jnp.bfloat16),
+            jax.ShapeDtypeStruct((2, frames, parts * rows + 2, cols, half), jnp.bfloat16),
+            jax.ShapeDtypeStruct((2, frames, rows + 2, cols, half), jnp.bfloat16),
+        ),
+        in_specs=[vmem] * 2,
+        out_specs=(vmem,) * 4,
+        scratch_shapes=[dma((messages,)), dma((messages,)), dma((4,))],
+        compiler_params=pltpu.CompilerParams(
+            collective_id=1, has_side_effects=True, vmem_limit_bytes=32 * 1024 * 1024
+        ),
+    )(act, grad)
+
+
+def split_over_space(latents, norm_gain, kernel, conv_bias, out_grad):
+    chans, half_cols = latents.shape[-1], kernel.shape[1]
+    _, frame_count, row_count, col_count = latents.shape[:4]
+    n_tm, n_space = lax.axis_size("tm"), lax.axis_size("space")
+    cell_total = frame_count * row_count * col_count * 2 * n_tm * n_space
+    grad_scale = 1.0 / math.sqrt(cell_total)
+    unit, per = chans // n_space, 27 * n_space // n_tm
+    slots = -(-per // n_space)
+
+    floats = latents.astype(jnp.float32)
+    scale = lax.rsqrt(jnp.mean(floats * floats, axis=-1, keepdims=True) + 1e-06)
+    normed = floats * scale
+    pre_act = normed * norm_gain
+    act = jax.nn.silu(pre_act).astype(jnp.bfloat16)
+    act_pair, act_rows, grad_rows, grad_next = exchange(act[0], out_grad[0], n_tm, n_space)
+
+    act_taps = tap_columns(pad_columns(act_pair), frame_count, row_count, col_count, False)
+    conv_part = jnp.dot(act_taps, kernel, preferred_element_type=jnp.float32)
+    conv_part = conv_part.reshape(2, frame_count, row_count, col_count, half_cols)
+    conv = lax.all_to_all(conv_part, "dp", split_axis=0, concat_axis=4, tiled=True)
+    block_out = (floats + conv + conv_bias).astype(jnp.bfloat16)
+
+    mine = lax.dynamic_slice_in_dim(
+        grad_rows, lax.axis_index("space") * row_count, row_count + 2, axis=2)
+    grad_ext = jnp.concatenate([mine, grad_next], axis=1)
+    flipped_kernel = jnp.transpose(kernel.reshape(-1, chans, half_cols), (0, 2, 1)).reshape(
+        -1, chans
+    )
+    grad_taps = tap_columns(pad_columns(grad_ext), frame_count, row_count, col_count, True)
+    partial_grad = jnp.dot(grad_taps, flipped_kernel, preferred_element_type=jnp.float32)
+    partial_grad = partial_grad.reshape(2, frame_count, row_count, col_count, chans)
+    act_grad = lax.psum_scatter(partial_grad, "dp", scatter_dimension=0, tiled=True)
+
+    grads = out_grad.astype(jnp.float32)
+    bias_local = jnp.sum(grads.reshape(-1, chans), axis=0) * grad_scale
+    sig = jax.nn.sigmoid(pre_act)
+    pre_grad = act_grad * sig * (1.0 + pre_act * (1.0 - sig))
+    gain_local = jnp.sum((pre_grad * normed).reshape(-1, chans), axis=0) * grad_scale
+    normed_grad = pre_grad * norm_gain
+    latent_grad = grads + scale * (
+        normed_grad - normed * jnp.mean(normed_grad * normed, axis=-1, keepdims=True)
+    )
+
+    wide = jnp.pad(grad_rows[:, :, 1:-1], ((0, 0), (0, 0), (0, 0), (1, 1), (0, 0)))
+    cot_rows = jnp.concatenate(
+        [wide[..., 2 - tap : 2 - tap + col_count, :] for tap in range(3)], axis=-1
+    ).reshape(2, -1, 3 * half_cols)
+    vec = jnp.concatenate([gain_local, bias_local]).reshape(-1, 128)
+    spread, vec = reduce_spread(
+        act_rows, cot_rows, vec, n_tm, n_space, per, slots, grad_scale)
+    kernel_grad = spread.reshape(-1, half_cols)[: per * unit].astype(jnp.float32)
+    gain_grad, bias_grad = vec.reshape(2, chans)
+    return (block_out, latent_grad.astype(jnp.bfloat16), kernel_grad, gain_grad, bias_grad)
 
 
 def on_device(latents, norm_gain, kernel, conv_bias, out_grad):
+    chans = latents.shape[-1]
+    n_tm, n_space = lax.axis_size("tm"), lax.axis_size("space")
+    splits = (
+        lax.axis_size("dp") == 2
+        and n_tm > 1
+        and n_space > 1
+        and latents.shape[:2] == (1, 2)
+        and chans % (128 * n_space) == 0
+        and chans % 256 == 0
+        and latents.shape[3] % 16 == 0
+        and 27 * n_space % n_tm == 0
+    )
+    path = split_over_space if splits else general
+    return path(latents, norm_gain, kernel, conv_bias, out_grad)
+
+
+def general(latents, norm_gain, kernel, conv_bias, out_grad):
     chans = latents.shape[-1]
     half_cols = kernel.shape[1]
     clip_local, frame_count, row_count, col_count = (
@@ -268,42 +633,15 @@
     conv_part = conv_part.reshape(pair_clips, frame_count, row_count, col_count, half_cols)
     conv = lax.all_to_all(conv_part, "dp", split_axis=0, concat_axis=4, tiled=True)
     block_out = (floats + conv + conv_bias).astype(jnp.bfloat16)
-    n_tm, n_space = lax.axis_size("tm"), lax.axis_size("space")
-    units = 27 * n_space
-    split = n_tm > 1 and n_space > 1 and chans % (128 * n_space) == 0 and units % n_tm == 0
-    if split:
-        unit, per = chans // n_space, units // n_tm
-        slots = -(-per // n_space)
-        act_part = lax.all_to_all(joined, "space", split_axis=4, concat_axis=2, tiled=True)
-        act_rows = lax.all_gather(act_part, "dp", axis=0, tiled=True)
-        act_rows = jnp.pad(act_rows, ((0, 0), (0, 0), (1, 1), (1, 1), (0, 0)))
-        grad_rows = lax.all_gather(grad_pair, "space", axis=2, tiled=True)
-        row_taps = tap_columns(act_rows, frame_count, row_count * n_space, col_count, False)
-        part = (
-            lax.dot_general(
-                row_taps,
-                grad_rows.reshape(-1, half_cols),
-                (((0,), (0,)), ((), ())),
-                preferred_element_type=jnp.float32,
-            )
-            * grad_scale
+    kernel_local = (
+        lax.dot_general(
+            act_taps,
+            grad_pair.reshape(-1, half_cols),
+            (((0,), (0,)), ((), ())),
+            preferred_element_type=jnp.float32,
         )
-        part = jnp.pad(part.reshape(27, unit, half_cols), ((0, 1), (0, 0), (0, 0)))
-        spread = reduce_spread(part, n_tm, n_space, per, slots)
-        kernel_grad = spread.reshape(-1, half_cols)[: per * unit].astype(jnp.float32)
-    else:
-        kernel_local = (
-            lax.dot_general(
-                act_taps,
-                grad_pair.reshape(-1, half_cols),
-                (((0,), (0,)), ((), ())),
-                preferred_element_type=jnp.float32,
-            )
-            * grad_scale
-        )
-        col_part = lax.psum_scatter(kernel_local, "space", scatter_dimension=1, tiled=True)
-        cell_part = lax.psum_scatter(col_part, "tm", scatter_dimension=0, tiled=True)
-        kernel_grad = lax.all_gather(cell_part, "space", axis=1, tiled=True)
+        * grad_scale
+    )
     flipped_kernel = jnp.transpose(kernel.reshape(-1, chans, half_cols), (0, 2, 1)).reshape(
         -1, chans
     )
@@ -321,6 +659,9 @@
         normed_grad - normed * jnp.mean(normed_grad * normed, axis=-1, keepdims=True)
     )
     gain_grad, bias_grad = lax.psum((gain_local, bias_local), ("dp", "tm", "space"))
+    col_part = lax.psum_scatter(kernel_local, "space", scatter_dimension=1, tiled=True)
+    cell_part = lax.psum_scatter(col_part, "tm", scatter_dimension=0, tiled=True)
+    kernel_grad = lax.all_gather(cell_part, "space", axis=1, tiled=True)
     return (block_out, latent_grad.astype(jnp.bfloat16), kernel_grad, gain_grad, bias_grad)
 
 

time: 268 us -> 232 us (0.87)
  blocking collectives: 70 us -> 0 us
  Pallas kernels: 43.9 us -> 99.8 us
  waiting for transfers between devices: 30.5 us -> 0.5 us
  local copies, waits for them, and re-layouts: 61.3 us -> 77.4 us
  starting transfers between devices: 16.8 us -> 3.87 us
  other arithmetic: 9.48 us -> 14.3 us
    psum x1 -> x0, blocking collectives: 44.3 us -> none  [on_device(): lax.psum((gain_local, bias_local), ('dp', 'tm', 'space'))]
    pallas_call x0 -> x1, Pallas kernels: none -> 39.2 us  [exchange(): pl.pallas_call(functools.partial(exchange_kernel, n, parts), out_shape=(j...]
    all_to_all x3 -> x0, blocking collectives: 25.7 us -> none  [the longest x1 17.2 us: on_device(): lax.all_to_all(joined, 'space', split_axis=4, concat_axis=2, tiled=True)]
    ppermute x6 -> x0, waiting for transfers between devices: 19 us -> none  [the longest x2 19 us: shifted(): return lax.ppermute(block, axis, route)]
    ppermute x6 -> x0, starting transfers between devices: 16.7 us -> none  [the longest x2 9.13 us: padded(): lax.ppermute(lax.slice_in_dim(block, block.shape[dim] - width, None, axis...]
    pallas_call x1, Pallas kernels: 43.9 us -> 60.6 us  [reduce_spread(): pl.pallas_call(functools.partial(reduce_spread_kernel, n, parts, per, slo...]
    unnamed x100 -> x75, local copies, waits for them, and re-layouts: 45.6 us -> 56.9 us
    reduce_scatter x1, waiting for transfers between devices: 10.7 us -> 0.01 us  [split_over_space(): lax.psum_scatter(partial_grad, 'dp', scatter_dimension=0, tiled=True)]
  transfers between devices with their start and end apart: 10 -> 2, of which waited for: 3 -> 1; matrix products, arithmetic and copies ran while one was open for 22% -> 20% of each run, Pallas kernels for 16% -> 0%
where the time goes in v2:
time: 232 us; the launch traced here: 231 us
  Pallas kernels  99.8 us (43%)
  local copies, waits for them, and re-layouts  77.4 us (33%)
  matrix products  20.7 us (9%)
  other arithmetic  14.3 us (6%)
  between operations  14.2 us (6%)
  starting transfers between devices  3.87 us (2%)
    pallas_call x1, Pallas kernels, reduce_spread(): pl.pallas_call(functools.partial(reduce_spread_kernel, n, parts, per, slo...  60.6 us
    unnamed x75, local copies, waits for them, and re-layouts  56.9 us
    pallas_call x1, Pallas kernels, exchange(): pl.pallas_call(functools.partial(exchange_kernel, n, parts), out_shape=(j...  39.2 us
    dot_general x1, matrix products, split_over_space(): jnp.dot(grad_taps, flipped_kernel, preferred_element_type=jnp.float32)  11.3 us
    transpose x1, local copies, waits for them, and re-layouts, split_over_space(): jnp.transpose(kernel.reshape(-1, chans, half_cols), (0, 2, 1))  10.3 us
    dot_general x1, matrix products, split_over_space(): conv_part = jnp.dot(act_taps, kernel, preferred_element_type=jnp.float32)  9.44 us
  transfers between devices with their start and end apart: 2, of which 1 were waited for; matrix products, arithmetic and copies ran while one was open for 20% of the time, Pallas kernels for 0%

profile of v2, /device:TPU:0, one launch (start us, length us, event | category | flops | bytes accessed | tf_op | source)
XLA Modules:
  0.0 230.8 jit_solution(5024543229019938461)
XLA Ops:
  8.4 1.2 fusion.23.act_ref
  10.6 39.2 %shard_map.92 = (bf16[2,4,4,80,512]{4,3,2,1,0:T(8,128)(2,1)S(1)}, bf16[2,4,10,80,128]{4,3,2,1,0:T(8,128)(2,1)S(1)}, bf16[2,2,10,80,256]{4,3,2,1,0:T(8,128)(2,1)S(1)}, bf16[2,2,4,80,256]{4,3,2,1,0:T(8,128)(2,1)S(1)}) custom-call(bf16[2,2,80,512]{3,2,1,0:T(8,128)(2,1)S(1)} %fusion.23.act_ref, bf16[2,2,80,512]{3,2,1,0:T(8,128)(2,1)S(1)} %bitcast.36), custom_call_target="tpu_custom_call" | custom-call | tf_op jit(solution)/shard_map/pallas_call | solution.py:509
  49.8 1.2 copy-done
  51.0 1.2 copy-done.2
  69.4 1.8 dynamic-slice_dynamic-update-slice_fusion.2
  71.2 1.8 slice_dynamic-update-slice_fusion.31
  73.0 1.8 slice_dynamic-update-slice_fusion.30
  74.8 1.7 dynamic-slice_dynamic-update-slice_fusion.1
  76.6 1.8 slice_dynamic-update-slice_fusion.29
  78.4 1.8 slice_dynamic-update-slice_fusion.28
  80.3 1.7 dynamic-slice_dynamic-update-slice_fusion
  82.0 1.9 slice_dynamic-update-slice_fusion.27
  83.9 10.3 %copy.11 = bf16[27,256,512]{2,1,0:T(8,128)(2,1)} copy(bf16[27,256,512]{1,2,0:T(8,128)(2,1)} %bitcast.38) | data formatting | bytes 14155776 | tf_op jit(solution)/shard_map/transpose | solution.py:551
  94.2 11.3 %fusion.30 = f32[2,2,2,80,512]{4,3,2,1,0:T(8,128)} fusion(bf16[2,2,2,80,6912]{4,3,2,1,0:T(8,128)(2,1)} %slice_dynamic-update-slice_fusion.27, bf16[6912,512,1,1,1]{1,0,4,3,2:T(8,128)(2,1)} %bitcast.41), kind=kOutput, calls=%fused_computation.105 | convolution fusion | flops 4529848320 | bytes 17235968 | tf_op jit(solution)/shard_map/dot_general | solution.py:555
  132.6 9.4 %fusion = f32[2,2,2,80,256]{4,3,2,1,0:T(8,128)} fusion(bf16[2,2,2,80,13824]{4,3,2,1,0:T(8,128)(2,1)} %slice_dynamic-update-slice_fusion, bf16[13824,256]{1,0:T(8,128)(2,1)S(1)} %bitcast.40), kind=kOutput, calls=%fused_computation | convolution fusion | flops 4529848320 | bytes 25427968 | tf_op jit(solution)/shard_map/dot_general | solution.py:543
  142.0 3.8 %all-to-all-start = ((f32[2,2,2,80,256]{4,3,2,1,0:T(8,128)}), f32[2,2,2,80,256]{4,3,2,1,0:T(8,128)S(1)}, u32[]{:S(2)}, u32[]{:S(2)}) async-start(f32[2,2,2,80,256]{4,3,2,1,0:T(8,128)} %fusion), calls=%async_computation | async-start | bytes 1310720 | tf_op jit(solution)/shard_map/all_to_all | solution.py:545
  145.9 1.2 slice.256
  148.4 3.4 %pad_slice_fusion.7 = (bf16[2,2,8,80,256]{4,3,2,1,0:T(8,128)(2,1)S(1)}, bf16[2,2,8,80,256]{4,3,2,1,0:T(8,128)(2,1)S(1)}) fusion(bf16[2,2,8,80,256]{4,3,2,1,0:T(8,128)(2,1)} %slice.256), kind=kLoop, calls=%fused_computation.12 | loop fusion | bytes 3932160 | tf_op jit(solution)/shard_map/slice | solution.py:571
  151.8 3.1 %pad_maximum_fusion = bf16[2,2,8,80,768]{4,3,2,1,0:T(8,128)(2,1)} fusion(bf16[2,2,8,80,256]{4,3,2,1,0:T(8,128)(2,1)S(1)} %get-tuple-element.20, bf16[2,2,8,80,256]{4,3,2,1,0:T(8,128)(2,1)} %slice.256, bf16[2,2,8,80,256]{4,3,2,1,0:T(8,128)(2,1)S(1)} %get-tuple-element.19), kind=kLoop, calls=%fused_computation.2 | loop fusion | flops 11796480 | bytes 7864320 | tf_op jit(solution)/shard_map/concatenate | solution.py:570
  154.9 1.6 fusion.19
  156.6 2.4 %convert_reduce_fusion = (f32[512]{0:T(512)S(1)}, bf16[1,2,2,80,512]{4,3,2,1,0:T(8,128)(2,1)}, bf16[1,2,2,80,512]{4,3,2,1,0:T(8,128)(2,1)}) fusion(bf16[1,2,2,80,512]{4,3,2,1,0:T(8,128)(2,1)S(1)} %copy-done.5, f32[2,2,80]{2,1,0:T(2,128)S(1)} %broadcast_multiply_fusion, f32[1,2,2,80,512]{4,3,2,1,0:T(8,128)} %reduce-scatter.2.cloned.1.call-done, ...), kind=kLoop, calls=%fused_computation.23 | loop fusion | flops 3603968 | bytes 2630144 | tf_op jit(solution)/shard_map/reduce_sum | solution.py:560
  159.1 1.4 copy-done.3
  160.5 60.6 %shard_map.93 = (bf16[28,128,256]{2,1,0:T(8,128)(2,1)S(1)}, f32[8,128]{1,0:T(8,128)S(1)}) custom-call(bf16[2,4,10,80,128]{4,3,2,1,0:T(8,128)(2,1)S(1)} %copy-done.3, bf16[2,1280,768]{2,1,0:T(8,128)(2,1)} %bitcast.37, f32[8,128]{1,0:T(8,128)S(1)} %pad_maximum_fusion.2.vec_ref), custom_call_target="tpu_custom_call" | custom-call | tf_op jit(solution)/shard_map/pallas_call | solution.py:263
  221.2 2.2 bitcast_convert_fusion
  (84 shorter events, 48.6 us)
Async XLA Ops:
  7.2 147.7 %reduce-scatter.2.cloned.1.call-start = ((), (), s32[]{:S(2)}) async-start(), calls=%async_computation.2 | async-start | bytes 1966080 | tf_op jit(solution)/shard_map/reduce_scatter | solution.py:557
  9.6 1.0 copy-start.4
  49.8 1.2 copy-start
  51.0 1.2 copy-start.2
  53.5 15.1 %copy-start.6 = (bf16[2,4,4,80,256]{4,3,2,1,0:T(8,128)(2,1)}, bf16[2,4,4,80,256]{4,3,2,1,0:T(8,128)(2,1)S(1)}, u32[]{:S(2)}) copy-start(bf16[2,4,4,80,256]{4,3,2,1,0:T(8,128)(2,1)S(1)} %pad_maximum_fusion.1) | copy-start | bytes 3932164
  125.4 7.1 %slice-start = ((s8[7077888]{0:T(1024)(128)(4,1)}), s8[4194304]{0:T(1024)(128)(4,1)S(1)}, s32[]{:S(2)}) async-start(s8[7077888]{0:T(1024)(128)(4,1)} %bitcast.39), calls=%async_computation.3 | async-start | bytes 8388608
  128.5 4.1 %slice-start.1 = ((s8[7077888]{0:T(1024)(128)(4,1)}), s8[2883584]{0:T(1024)(128)(4,1)S(1)}, s32[]{:S(2)}) async-start(s8[7077888]{0:T(1024)(128)(4,1)} %bitcast.39), calls=%async_computation.4 | async-start | bytes 5767168
  132.6 13.3 %copy-start.1 = (bf16[2,2,10,80,256]{4,3,2,1,0:T(8,128)(2,1)S(1)}, bf16[2,2,10,80,256]{4,3,2,1,0:T(8,128)(2,1)}, u32[]{:S(2)}) copy-start(bf16[2,2,10,80,256]{4,3,2,1,0:T(8,128)(2,1)} %copy-done) | copy-start | bytes 4915204
  142.0 12.9 %copy-start.7 = (bf16[1,2,2,80,512]{4,3,2,1,0:T(8,128)(2,1)S(1)}, bf16[1,2,2,80,512]{4,3,2,1,0:T(8,128)(2,1)}, u32[]{:S(2)}) copy-start(bf16[1,2,2,80,512]{4,3,2,1,0:T(8,128)(2,1)} %param.5) | copy-start | bytes 983044
  142.0 12.9 %copy-start.9 = (f32[512]{0:T(512)S(1)}, f32[512]{0:T(512)}, u32[]{:S(2)}) copy-start(f32[512]{0:T(512)} %param.6) | copy-start | bytes 6148
  142.0 14.6 %copy-start.5 = (bf16[1,2,2,80,512]{4,3,2,1,0:T(8,128)(2,1)S(1)}, bf16[1,2,2,80,512]{4,3,2,1,0:T(8,128)(2,1)}, u32[]{:S(2)}) copy-start(bf16[1,2,2,80,512]{4,3,2,1,0:T(8,128)(2,1)} %param.9) | copy-start | bytes 983044
  142.0 14.6 %copy-start.10 = (f32[512]{0:T(512)S(1)}, f32[512]{0:T(512)}, u32[]{:S(2)}) copy-start(f32[512]{0:T(512)} %param.8) | copy-start | bytes 6148
  142.0 5.5 %all-to-all-start = ((f32[2,2,2,80,256]{4,3,2,1,0:T(8,128)}), f32[2,2,2,80,256]{4,3,2,1,0:T(8,128)S(1)}, u32[]{:S(2)}, u32[]{:S(2)}) async-start(f32[2,2,2,80,256]{4,3,2,1,0:T(8,128)} %fusion), calls=%async_computation | async-start | bytes 1310720 | tf_op jit(solution)/shard_map/all_to_all | solution.py:545
  148.4 8.1 %copy-start.8 = (f32[1,2,2,2,10,8,256]{6,5,1,4,3,2,0:T(8,128)S(1)}, f32[1,2,2,2,10,8,256]{6,5,1,4,3,2,0:T(8,128)}, u32[]{:S(2)}) copy-start(f32[1,2,2,2,10,8,256]{6,5,1,4,3,2,0:T(8,128)} %copy.14) | copy-start | bytes 1966084
  159.0 1.4 copy-start.3
Sparse Core Ops, SparseCore 0:
  105.6 16.5 reduce-scatter.1

commit v3 on v2

--- a/solution.py
+++ b/solution.py
@@ -77,12 +77,24 @@
     return me_d, me_t, me_s
 
 
-def reduce_spread_kernel(
-    n, parts, per, slots, grad_scale, act_ref, cot_ref, vec_ref, out_ref, vec_out,
-    part_ref, from_left, from_right, to_right, to_left, done, vec_plane, vec_line, vec_pair,
+def shift_columns(block, distance, cols):
+    rolled = pltpu.roll(block, distance % block.shape[0], axis=0)
+    col = lax.rem(lax.broadcasted_iota(jnp.int32, block.shape, 0), cols)
+    edge = 0 if distance > 0 else cols - 1
+    return jnp.where(col == edge, 0.0, rolled)
+
+
+def block_kernel(
+    n, parts, per, slots, grad_scale,
+    act_ref, pair_ref, rows_ref, next_ref, lat_ref, cot_ref, gain_ref, bias_ref, kernel_hbm,
+    out_ref, block_out, latent_grad, vec_out,
+    part_ref, from_left, from_right, to_right, to_left, done, vec_ref, vec_plane, vec_line, vec_pair,
+    wide_ref, ext_ref, weights, conv_acc, back_acc, conv_mine, conv_send, back_mine, back_send, back_got,
     right_send, right_recv, left_send, left_recv, spread_send, spread_recv, own_sem,
-    plane_send, plane_recv, line_send, line_recv, pair_send, pair_recv,
+    plane_send, plane_recv, line_send, line_recv, pair_send, pair_recv, swap_send, swap_recv, load_sem,
 ):
+    load = pltpu.make_async_copy(kernel_hbm, weights, load_sem)
+    load.start()
     me_d, me_t, me_s = greet(n, parts)
     half = out_ref.shape[-1]
     frames, rows = act_ref.shape[1] // 2, act_ref.shape[2] - 2
@@ -104,31 +116,104 @@
         send_sem=pair_send, recv_sem=pair_recv,
         device_id=(1 - me_d, me_t, me_s), device_id_type=MESH)
 
-    for other in range(1, parts):
-        plane_copy(other).start()
-    vec_plane[me_s] = vec_ref[...]
-
-    for tap_t in range(3):
-        for tap_h in range(3):
-            total = None
-            for clip in range(2):
-                window = act_ref[clip, tap_t : tap_t + frames, tap_h : tap_h + rows]
-                term = lax.dot_general(
-                    window.reshape(-1, window.shape[-1]), cot_ref[clip],
-                    (((0,), (0,)), ((), ())), preferred_element_type=jnp.float32)
-                total = term if total is None else total + term
-            total = total * grad_scale
-            for tap_w in range(3):
-                part_ref[9 * tap_t + 3 * tap_h + tap_w] = total[
-                    :, tap_w * half : (tap_w + 1) * half
-                ]
+    cols = act_ref.shape[3]
+    own_rows = conv_send.shape[0]
+    for clip in range(2):
+        flat = rows_ref[clip, :, 1 : 1 + rows].reshape(-1, half)
+        exact = flat.astype(jnp.float32)
+        wide_ref[clip, :, 0:half] = shift_columns(exact, -1, cols).astype(jnp.bfloat16)
+        wide_ref[clip, :, half : 2 * half] = flat
+        wide_ref[clip, :, 2 * half :] = shift_columns(exact, 1, cols).astype(jnp.bfloat16)
+
+    def tap_row(group):
+        tap_t, tap_h = divmod(group, 3)
+        total = None
+        for clip in range(2):
+            window = act_ref[clip, tap_t : tap_t + frames, tap_h : tap_h + rows]
+            term = lax.dot_general(
+                window.reshape(-1, window.shape[-1]), wide_ref[clip],
+                (((0,), (0,)), ((), ())), preferred_element_type=jnp.float32)
+            total = term if total is None else total + term
+        total = total * grad_scale
+        for tap_w in range(3):
+            part_ref[3 * group + tap_w] = total[:, tap_w * half : (tap_w + 1) * half]
+
+    needed = {}
+    for dest in range(n):
+        for quarter in range(parts):
+            for slot in range(slots):
+                group = (first_tap(dest, quarter, per, parts) + slot) // 3
+                needed[group] = min(slot, needed.get(group, slots))
+    for group in range(9):
+        if needed[group] == 0:
+            tap_row(group)
     part_ref[27] = jnp.zeros_like(part_ref[27])
 
-    for other in range(1, parts):
-        plane_copy(other).wait()
-    vec_line[me_t] = functools.reduce(lambda a, b: a + b, [vec_plane[i] for i in range(parts)])
-    for other in range(1, n):
-        line_copy(other).start()
+    small = ext_ref.shape[2]
+    ext_ref[:, 0:frames] = rows_ref[:, :, pl.ds(me_s * (small - 2), small)]
+    ext_ref[:, frames:] = next_ref[...]
+    conv_acc[...] = jnp.zeros_like(conv_acc)
+    back_acc[...] = jnp.zeros_like(back_acc)
+
+    def conv_step(group):
+        tap_t, tap_h = lax.div(group, 3), lax.rem(group, 3)
+        window = pair_ref[:, pl.ds(tap_t, frames), pl.ds(tap_h, small - 2)]
+        window = window.reshape(-1, window.shape[-1])
+        back = ext_ref[:, pl.ds(2 - tap_t, frames), pl.ds(2 - tap_h, small - 2)]
+        back = back.reshape(-1, half)
+        for tap_w in range(3):
+            block = weights[3 * group + tap_w]
+            conv_acc[tap_w] += jnp.dot(window, block, preferred_element_type=jnp.float32)
+            back_acc[tap_w] += lax.dot_general(
+                back, block, (((1,), (1,)), ((), ())), preferred_element_type=jnp.float32)
+
+    def clip_sum(acc, clip, sign):
+        at = pl.ds(pl.multiple_of(clip * own_rows, own_rows), own_rows)
+        return (
+            shift_columns(acc[0, at], sign, cols)
+            + acc[1, at]
+            + shift_columns(acc[2, at], -sign, cols)
+        )
+
+    conv_swap = pltpu.make_async_remote_copy(
+        src_ref=conv_send, dst_ref=conv_mine.at[me_d],
+        send_sem=swap_send.at[0], recv_sem=swap_recv.at[0],
+        device_id=(1 - me_d, me_t, me_s), device_id_type=MESH)
+    back_swap = pltpu.make_async_remote_copy(
+        src_ref=back_send, dst_ref=back_got,
+        send_sem=swap_send.at[1], recv_sem=swap_recv.at[1],
+        device_id=(1 - me_d, me_t, me_s), device_id_type=MESH)
+
+    def start_swaps():
+        conv_send[...] = clip_sum(conv_acc, 1 - me_d, 1)
+        conv_swap.start()
+        back_send[...] = clip_sum(back_acc, 1 - me_d, -1)
+        back_swap.start()
+        conv_mine[me_d] = clip_sum(conv_acc, me_d, 1)
+        back_mine[...] = clip_sum(back_acc, me_d, -1)
+
+    def finish():
+        floats = lat_ref[...].astype(jnp.float32)
+        grads = cot_ref[...].astype(jnp.float32)
+        gain = gain_ref[...]
+        conv_swap.wait()
+        back_swap.wait()
+        conv = jnp.concatenate([conv_mine[0], conv_mine[1]], axis=-1)
+        block_out[...] = (floats + conv + bias_ref[...]).astype(jnp.bfloat16)
+        scale = lax.rsqrt(jnp.mean(floats * floats, axis=-1, keepdims=True) + 1e-06)
+        normed = floats * scale
+        pre_act = normed * gain
+        sig = 1.0 / (1.0 + jnp.exp(-pre_act))
+        pre_grad = (back_mine[...] + back_got[...]) * sig * (1.0 + pre_act * (1.0 - sig))
+        normed_grad = pre_grad * gain
+        inner = jnp.mean(normed_grad * normed, axis=-1, keepdims=True)
+        latent_grad[...] = (grads + scale * (normed_grad - normed * inner)).astype(jnp.bfloat16)
+        vec_ref[...] = jnp.zeros_like(vec_ref)
+        vec_ref[0:1] = jnp.sum(pre_grad * normed, axis=0, keepdims=True) * grad_scale
+        vec_ref[1:2] = jnp.sum(grads, axis=0, keepdims=True) * grad_scale
+        for other in range(1, parts):
+            plane_copy(other).start()
+        vec_plane[me_s] = vec_ref[...]
 
     def mine(dest, slot):
         return part_ref[first_tap(dest, me_s, per, parts) + slot]
@@ -192,7 +277,7 @@
 
                 left_copy(dest_l, l_slot, me_t - 1).start()
 
-        @pl.when(f_slot >= 0)
+        @pl.when((f_slot >= 0) & (f_slot < slots))
         def _():
             @pl.when(me_t == 0)
             def _():
@@ -224,10 +309,24 @@
                 done.at[f_slot], out_ref.at[parts * f_slot + offset], own_sem.at[f_slot]
             ).start()
 
+        for group in range(9):
+            if needed[group] > 0:
+                pl.when(it == needed[group] - 1)(functools.partial(tap_row, group))
+
+        pl.when(it == 0)(load.wait)
+        pl.when(it < 9)(lambda: conv_step(it))
+        pl.when(it == last - 1)(start_swaps)
+        pl.when(it == last)(finish)
         return carry
 
-    lax.fori_loop(0, n + slots, step, 0)
-
+    last = max(n + slots - 1, 10)
+    lax.fori_loop(0, last + 1, step, 0)
+
+    for other in range(1, parts):
+        plane_copy(other).wait()
+    vec_line[me_t] = functools.reduce(lambda a, b: a + b, [vec_plane[i] for i in range(parts)])
+    for other in range(1, n):
+        line_copy(other).start()
     for other in range(1, n):
         line_copy(other).wait()
     vec_pair[0] = functools.reduce(lambda a, b: a + b, [vec_line[i] for i in range(n)])
@@ -255,37 +354,58 @@
     vec_out[...] = vec_pair[0] + vec_pair[1]
 
 
-def reduce_spread(act_rows, cot_rows, vec, n, parts, per, slots, grad_scale):
-    unit, cols = act_rows.shape[-1], cot_rows.shape[-1] // 3
+def whole_block(
+    act_rows, act_pair, grad_rows, grad_next, latents, out_grad, gain, bias, kernel,
+    n, parts, per, slots, grad_scale,
+):
+    unit, cols = act_rows.shape[-1], kernel.shape[-1]
+    chans = latents.shape[-1]
+    cells = latents.shape[0]
+    frames, all_rows, width = grad_rows.shape[1], grad_rows.shape[2] - 2, grad_rows.shape[3]
     block = (n, slots, unit, cols)
     dma = pltpu.SemaphoreType.DMA
     vmem = pl.BlockSpec(memory_space=pltpu.VMEM)
+    low, full = jnp.bfloat16, jnp.float32
     return pl.pallas_call(
-        functools.partial(reduce_spread_kernel, n, parts, per, slots, grad_scale),
+        functools.partial(block_kernel, n, parts, per, slots, grad_scale),
         out_shape=(
-            jax.ShapeDtypeStruct((parts * slots, unit, cols), jnp.bfloat16),
-            jax.ShapeDtypeStruct(vec.shape, jnp.float32),
+            jax.ShapeDtypeStruct((parts * slots, unit, cols), low),
+            jax.ShapeDtypeStruct((cells, chans), low),
+            jax.ShapeDtypeStruct((cells, chans), low),
+            jax.ShapeDtypeStruct((8, chans), full),
         ),
-        in_specs=[vmem] * 3,
-        out_specs=(vmem, vmem),
-        scratch_shapes=[pltpu.VMEM((28, unit, cols), jnp.float32)]
-        + [pltpu.VMEM(block, jnp.bfloat16)] * 4
+        in_specs=[vmem] * 8 + [pl.BlockSpec(memory_space=pl.ANY)],
+        out_specs=(vmem,) * 4,
+        scratch_shapes=[pltpu.VMEM((28, unit, cols), full)]
+        + [pltpu.VMEM(block, low)] * 4
         + [
-            pltpu.VMEM((slots, unit, cols), jnp.bfloat16),
-            pltpu.VMEM((parts,) + vec.shape, jnp.float32),
-            pltpu.VMEM((n,) + vec.shape, jnp.float32),
-            pltpu.VMEM((2,) + vec.shape, jnp.float32),
+            pltpu.VMEM((slots, unit, cols), low),
+            pltpu.VMEM((8, chans), full),
+            pltpu.VMEM((parts, 8, chans), full),
+            pltpu.VMEM((n, 8, chans), full),
+            pltpu.VMEM((2, 8, chans), full),
+            pltpu.VMEM((2, frames * all_rows * width, 3 * cols), low),
+            pltpu.VMEM((2, 2 * frames) + grad_next.shape[2:], low),
+            pltpu.VMEM(kernel.shape, low),
+            pltpu.VMEM((3, 2 * cells, cols), full),
+            pltpu.VMEM((3, 2 * cells, chans), full),
+            pltpu.VMEM((2, cells, cols), full),
+            pltpu.VMEM((cells, cols), full),
+            pltpu.VMEM((cells, chans), full),
+            pltpu.VMEM((cells, chans), full),
+            pltpu.VMEM((cells, chans), full),
         ]
         + [dma((n, slots))] * 4
         + [dma((parts - 1, slots))] * 2
         + [dma((slots,))]
         + [dma((parts - 1,))] * 2
         + [dma((n - 1,))] * 2
-        + [dma, dma],
+        + [dma, dma]
+        + [dma((2,)), dma((2,)), dma],
         compiler_params=pltpu.CompilerParams(
-            collective_id=0, has_side_effects=True, vmem_limit_bytes=48 * 1024 * 1024
+            collective_id=0, has_side_effects=True, vmem_limit_bytes=60 * 1024 * 1024
         ),
-    )(act_rows, cot_rows, vec)
+    )(act_rows, act_pair, grad_rows, grad_next, latents, out_grad, gain, bias, kernel)
 
 
 def exchange_kernel(n, parts, act_ref, grad_ref, af, aq, gr, gn, send, recv, local):
@@ -534,48 +654,17 @@
 
     floats = latents.astype(jnp.float32)
     scale = lax.rsqrt(jnp.mean(floats * floats, axis=-1, keepdims=True) + 1e-06)
-    normed = floats * scale
-    pre_act = normed * norm_gain
-    act = jax.nn.silu(pre_act).astype(jnp.bfloat16)
+    act = jax.nn.silu(floats * scale * norm_gain).astype(jnp.bfloat16)
     act_pair, act_rows, grad_rows, grad_next = exchange(act[0], out_grad[0], n_tm, n_space)
-
-    act_taps = tap_columns(pad_columns(act_pair), frame_count, row_count, col_count, False)
-    conv_part = jnp.dot(act_taps, kernel, preferred_element_type=jnp.float32)
-    conv_part = conv_part.reshape(2, frame_count, row_count, col_count, half_cols)
-    conv = lax.all_to_all(conv_part, "dp", split_axis=0, concat_axis=4, tiled=True)
-    block_out = (floats + conv + conv_bias).astype(jnp.bfloat16)
-
-    mine = lax.dynamic_slice_in_dim(
-        grad_rows, lax.axis_index("space") * row_count, row_count + 2, axis=2)
-    grad_ext = jnp.concatenate([mine, grad_next], axis=1)
-    flipped_kernel = jnp.transpose(kernel.reshape(-1, chans, half_cols), (0, 2, 1)).reshape(
-        -1, chans
-    )
-    grad_taps = tap_columns(pad_columns(grad_ext), frame_count, row_count, col_count, True)
-    partial_grad = jnp.dot(grad_taps, flipped_kernel, preferred_element_type=jnp.float32)
-    partial_grad = partial_grad.reshape(2, frame_count, row_count, col_count, chans)
-    act_grad = lax.psum_scatter(partial_grad, "dp", scatter_dimension=0, tiled=True)
-
-    grads = out_grad.astype(jnp.float32)
-    bias_local = jnp.sum(grads.reshape(-1, chans), axis=0) * grad_scale
-    sig = jax.nn.sigmoid(pre_act)
-    pre_grad = act_grad * sig * (1.0 + pre_act * (1.0 - sig))
-    gain_local = jnp.sum((pre_grad * normed).reshape(-1, chans), axis=0) * grad_scale
-    normed_grad = pre_grad * norm_gain
-    latent_grad = grads + scale * (
-        normed_grad - normed * jnp.mean(normed_grad * normed, axis=-1, keepdims=True)
-    )
-
-    wide = jnp.pad(grad_rows[:, :, 1:-1], ((0, 0), (0, 0), (0, 0), (1, 1), (0, 0)))
-    cot_rows = jnp.concatenate(
-        [wide[..., 2 - tap : 2 - tap + col_count, :] for tap in range(3)], axis=-1
-    ).reshape(2, -1, 3 * half_cols)
-    vec = jnp.concatenate([gain_local, bias_local]).reshape(-1, 128)
-    spread, vec = reduce_spread(
-        act_rows, cot_rows, vec, n_tm, n_space, per, slots, grad_scale)
+    spread, block_out, latent_grad, vec = whole_block(
+        act_rows, act_pair, grad_rows, grad_next,
+        latents.reshape(-1, chans), out_grad.reshape(-1, chans),
+        norm_gain.reshape(1, chans), conv_bias.reshape(1, chans),
+        kernel.reshape(27, chans, half_cols), n_tm, n_space, per, slots, grad_scale)
     kernel_grad = spread.reshape(-1, half_cols)[: per * unit].astype(jnp.float32)
-    gain_grad, bias_grad = vec.reshape(2, chans)
-    return (block_out, latent_grad.astype(jnp.bfloat16), kernel_grad, gain_grad, bias_grad)
+    return (
+        block_out.reshape(latents.shape), latent_grad.reshape(latents.shape), kernel_grad,
+        vec[0], vec[1])
 
 
 def on_device(latents, norm_gain, kernel, conv_bias, out_grad):

time: 232 us -> 123 us (0.53)
  local copies, waits for them, and re-layouts: 77.4 us -> 10.1 us
  matrix products: 20.7 us -> 0 us
  between operations: 14.2 us -> 0.71 us
  other arithmetic: 14.3 us -> 4.56 us
  Pallas kernels: 99.8 us -> 107 us
  starting transfers between devices: 3.87 us -> 0 us
    unnamed x75 -> x16, local copies, waits for them, and re-layouts: 56.9 us -> 7.14 us
    dot_general x2 -> x0, matrix products: 20.7 us -> none  [the longest x1 11.3 us: split_over_space(): jnp.dot(grad_taps, flipped_kernel, preferred_element_type=jnp.float32)]
    transpose x1 -> x0, local copies, waits for them, and re-layouts: 10.3 us -> none  [split_over_space(): jnp.transpose(kernel.reshape(-1, chans, half_cols), (0, 2, 1))]
    pallas_call x1, Pallas kernels: 60.6 us -> 68.1 us  [whole_block(): pl.pallas_call(functools.partial(block_kernel, n, parts, per, slots, grad...]
    reduce_sum x2 -> x0, other arithmetic: 4.07 us -> none  [the longest x1 2.44 us: split_over_space(): bias_local = jnp.sum(grads.reshape(-1, chans), axis=0) * grad_scale]
    all_to_all x1 -> x0, starting transfers between devices: 3.83 us -> none  [split_over_space(): lax.all_to_all(conv_part, 'dp', split_axis=0, concat_axis=4, tiled=True)]
    concatenate x3 -> x0, other arithmetic: 3.21 us -> none  [the longest x1 3.09 us: split_over_space(): jnp.concatenate([wide[..., 2 - tap:2 - tap + col_count, :] for tap in ran...]
    slice x2 -> x1, local copies, waits for them, and re-layouts: 4.53 us -> 1.38 us  [split_over_space(): vec[1]]
  transfers between devices with their start and end apart: 2 -> 0, of which waited for: 1 -> 0; matrix products, arithmetic and copies ran while one was open for 20% -> 0% of each run, Pallas kernels for 0% -> 0%
where the time goes in v3:
time: 123 us
  Pallas kernels  107 us (87%)
  local copies, waits for them, and re-layouts  10.1 us (8%)
  other arithmetic  4.56 us (4%)
    pallas_call x1, Pallas kernels, whole_block(): pl.pallas_call(functools.partial(block_kernel, n, parts, per, slots, grad...  68.1 us
    pallas_call x1, Pallas kernels, exchange(): pl.pallas_call(functools.partial(exchange_kernel, n, parts), out_shape=(j...  39.2 us
    unnamed x16, local copies, waits for them, and re-layouts  7.14 us

profile of v3, /device:TPU:0, one launch (start us, length us, event | category | flops | bytes accessed | tf_op | source)
XLA Modules:
  0.0 122.7 jit_solution(4675031604043819112)
XLA Ops:
  0.6 1.1 fusion
  1.8 1.2 %fusion.8.act_ref = bf16[2,2,80,512]{3,2,1,0:T(8,128)(2,1)S(1)} fusion(bf16[1,2,2,80,512]{4,3,2,1,0:T(8,128)(2,1)} %param.5, f32[512]{0:T(512)} %param.6, f32[2,2,80]{2,1,0:T(2,128)S(1)} %add_rsqrt_fusion), kind=kLoop, calls=%fused_computation.11 | loop fusion | flops 1310720 | bytes 658688 | tf_op jit(solution)/shard_map/squeeze | solution.py:658
  3.0 0.0 copy-start.3
  3.0 1.0 copy-done.3
  4.0 39.2 %shard_map.92 = (bf16[2,4,4,80,512]{4,3,2,1,0:T(8,128)(2,1)S(1)}, bf16[2,4,10,80,128]{4,3,2,1,0:T(8,128)(2,1)S(1)}, bf16[2,2,10,80,256]{4,3,2,1,0:T(8,128)(2,1)S(1)}, bf16[2,2,4,80,256]{4,3,2,1,0:T(8,128)(2,1)S(1)}) custom-call(bf16[2,2,80,512]{3,2,1,0:T(8,128)(2,1)S(1)} %fusion.8.act_ref, bf16[2,2,80,512]{3,2,1,0:T(8,128)(2,1)S(1)} %bitcast.16), custom_call_target="tpu_custom_call" | custom-call | tf_op jit(solution)/shard_map/pallas_call | solution.py:629
  43.2 0.0 copy-start
  43.3 1.5 %copy-done = bf16[2,4,4,80,512]{4,3,2,1,0:T(8,128)(2,1)} copy-done((bf16[2,4,4,80,512]{4,3,2,1,0:T(8,128)(2,1)}, bf16[2,4,4,80,512]{4,3,2,1,0:T(8,128)(2,1)S(1)}, u32[]{:S(2)}) %copy-start) | copy-done | bytes 2621464
  44.7 0.0 copy-start.1
  44.7 1.2 copy-done.1
  45.9 0.0 copy-start.2
  45.9 1.2 copy-done.2
  47.1 0.0 copy-start.4
  47.1 0.9 copy-done.4
  48.0 68.1 %shard_map.93 = (bf16[28,128,256]{2,1,0:T(8,128)(2,1)}, bf16[320,512]{1,0:T(8,128)(2,1)}, bf16[320,512]{1,0:T(8,128)(2,1)}, f32[8,512]{1,0:T(8,128)}) custom-call(bf16[2,4,10,80,128]{4,3,2,1,0:T(8,128)(2,1)} %copy-done.1, bf16[2,4,4,80,512]{4,3,2,1,0:T(8,128)(2,1)} %copy-done, bf16[2,2,10,80,256]{4,3,2,1,0:T(8,128)(2,1)} %copy-done.2, ...), custom_call_target="tpu_custom_call" | custom-call | tf_op jit(solution)/shard_map/pallas_call | solution.py:369
  116.1 1.4 %fusion.9 = (f32[1,512]{1,0:T(1,128)}, f32[1,512]{1,0:T(1,128)}) fusion(f32[8,512]{1,0:T(8,128)} %get-tuple-element.20), kind=kLoop, calls=%fused_computation.13 | loop fusion | bytes 8192 | tf_op jit(solution)/shard_map/slice | solution.py:667
  117.4 1.6 %slice.10 = bf16[27,128,256]{2,1,0:T(8,128)(2,1)S(1)} slice(bf16[28,128,256]{2,1,0:T(8,128)(2,1)} %get-tuple-element.19), slice={[0:27], [0:128], [0:256]} | slice | bytes 3538944 | tf_op jit(solution)/shard_map/slice | solution.py:664
  119.0 0.0 copy-start.6
  119.0 0.0 copy-start.5
  119.1 2.2 %bitcast_convert_fusion = f32[3456,256]{1,0:T(8,128)} fusion(bf16[27,128,256]{2,1,0:T(8,128)(2,1)S(1)} %slice.10), kind=kLoop, calls=%fused_computation | loop fusion | flops 884736 | bytes 5308416 | tf_op jit(solution)/shard_map/convert_element_type | solution.py:664
  121.2 0.0 copy-done.6
  121.2 0.7 copy.12
  122.0 0.0 copy-done.5
  122.0 0.7 copy.13
  (1 shorter events, 0.0 us)
Async XLA Ops:
  3.0 1.0 copy-start.3
  43.2 1.5 %copy-start = (bf16[2,4,4,80,512]{4,3,2,1,0:T(8,128)(2,1)}, bf16[2,4,4,80,512]{4,3,2,1,0:T(8,128)(2,1)S(1)}, u32[]{:S(2)}) copy-start(bf16[2,4,4,80,512]{4,3,2,1,0:T(8,128)(2,1)S(1)} %get-tuple-element.14.pair_ref) | copy-start | bytes 7864324
  44.7 1.2 copy-start.1
  45.9 1.2 copy-start.2
  47.1 0.9 copy-start.4
  119.0 2.2 %copy-start.6 = (bf16[320,512]{1,0:T(8,128)(2,1)S(1)}, bf16[320,512]{1,0:T(8,128)(2,1)}, u32[]{:S(2)}) copy-start(bf16[320,512]{1,0:T(8,128)(2,1)} %get-tuple-element.17) | copy-start | bytes 983044
  119.0 2.9 %copy-start.5 = (bf16[320,512]{1,0:T(8,128)(2,1)S(1)}, bf16[320,512]{1,0:T(8,128)(2,1)}, u32[]{:S(2)}) copy-start(bf16[320,512]{1,0:T(8,128)(2,1)} %get-tuple-element.18) | copy-start | bytes 983044
